TPU v7x, 32 devices: a whole 2x2x4 slice. The times are simulated.
32 devices in a mesh: dp: 4 (over z), tile: 4 (over x, core), seq: 2 (over y).
Axes of the slice: x: 2, y: 2, z: 4, core: 2. Of those that a mesh axis runs over, the one named last changes fastest.
Arguments:
- features: bfloat16 [4, 8, 16, 32, 128], P('dp', None, 'tile'), may hold values from -6 to 6
- lengths: int32 [4], P('dp'), may hold values from 1 to 8, as said below
- weight: bfloat16 [3456, 5120], P(('dp', 'tile'), 'seq'), may hold values from -0.109375 to 0.109375
- bias: bfloat16 [5120], P('seq'), may hold values from -3 to 3
- cotangent: bfloat16 [4, 8, 16, 32, 5120], P('dp', 'seq', 'tile'), may hold values from -6 to 6
Outputs:
- pose_tokens: bfloat16 [4, 8, 16, 32, 5120], P('dp', 'seq', 'tile')
- grad_features: bfloat16 [4, 8, 16, 32, 128], P('dp', None, 'tile')
- grad_weight: float32 [3456, 5120], P(('dp', 'tile'), 'seq')
- grad_bias: float32 [5120], P('seq')
Inputs may be any that keep to these rules, and one draw needn't show every extreme that they name: `lengths`: exactly one clip has 8 live frames; every other clip has at most 4.
All inputs are finite; a program needn't handle non-finite values.
Results may differ from a plain program's by a relative error of at most 0.005.
Values may be sent and summed in bfloat16 or wider, within the bound.
A program may use at most 512 MiB of HBM per device.

v0:
```python
import jax
import jax.numpy as jnp
from jax import lax
from jax.sharding import PartitionSpec as P


def extended(block, sides, width):
    for axis, dim in sides:
        count = lax.axis_size(axis)
        forward = [(i, i + 1) for i in range(count - 1)]
        backward = [(target, source) for source, target in forward]
        low = lax.ppermute(
            lax.slice_in_dim(block, block.shape[dim] - width, None, axis=dim), axis, forward
        )
        high = lax.ppermute(lax.slice_in_dim(block, 0, width, axis=dim), axis, backward)
        block = jnp.concatenate([low, block, high], axis=dim)
    return block


def silu_grad(values):
    sigma = jax.nn.sigmoid(values)
    return sigma * (1.0 + values * (1.0 - sigma))


def tap_block(padded, start_f, start_h, start_w, frame_count, row_count, col_count):
    block = padded[
        start_f : start_f + frame_count,
        start_h : start_h + row_count,
        start_w : start_w + col_count,
    ]
    return block.reshape(frame_count * row_count * col_count, padded.shape[3])


def shards(features, lengths, weight, bias, cotangent):
    local_feat = features[0]
    frame_count, row_count, col_count, chan_count = local_feat.shape
    row_total = frame_count * row_count * col_count
    frame_mask = (jnp.arange(frame_count) < lengths[0]).astype(jnp.float32)[:, None, None, None]
    inner_vals = local_feat.astype(jnp.float32)
    hidden = (jax.nn.silu(inner_vals) * frame_mask).astype(jnp.bfloat16)
    full_weight = lax.all_gather(weight, ("dp", "tile"), axis=0, tiled=True)
    width_share = full_weight.shape[1]
    kernel = full_weight.reshape(27, chan_count, width_share)
    with_rims = extended(hidden, (("tile", 1),), 1)
    padded_feat = jnp.pad(with_rims, ((1, 1), (0, 0), (1, 1), (0, 0)))
    output = jnp.zeros((row_total, width_share), jnp.float32)
    for tap_f in range(3):
        for tap_h in range(3):
            for tap_w in range(3):
                index = (tap_f * 3 + tap_h) * 3 + tap_w
                columns = tap_block(
                    padded_feat, tap_f, tap_h, tap_w, frame_count, row_count, col_count
                )
                output = output + jnp.dot(
                    columns, kernel[index], preferred_element_type=jnp.float32
                )
    channel_tokens = (
        (output.reshape(frame_count, row_count, col_count, width_share) + bias.astype(jnp.float32))
        * frame_mask
    ).astype(jnp.bfloat16)
    pose_tokens = lax.all_to_all(channel_tokens, "seq", split_axis=0, concat_axis=3, tiled=True)
    grad_channels = lax.all_to_all(cotangent[0], "seq", split_axis=3, concat_axis=0, tiled=True)
    grad_out = grad_channels * frame_mask.astype(jnp.bfloat16)
    flat_grad = grad_out.reshape(row_total, width_share)
    pieces = []
    for tap_f in range(3):
        for tap_h in range(3):
            for tap_w in range(3):
                columns = tap_block(
                    padded_feat, tap_f, tap_h, tap_w, frame_count, row_count, col_count
                )
                pieces.append(
                    lax.dot_general(
                        columns,
                        flat_grad,
                        (((0,), (0,)), ((), ())),
                        preferred_element_type=jnp.float32,
                    )
                )
    weight_term = jnp.concatenate(pieces, 0)
    bias_term = jnp.sum(flat_grad, axis=0, dtype=jnp.float32)
    grad_weight = lax.psum_scatter(weight_term, ("dp", "tile"), scatter_dimension=0, tiled=True)
    grad_bias = lax.psum(bias_term, ("dp", "tile"))
    grad_rims = extended(grad_out, (("tile", 1),), 1)
    padded_grad = jnp.pad(grad_rims, ((1, 1), (0, 0), (1, 1), (0, 0)))
    partial_flat = jnp.zeros((row_total, chan_count), jnp.float32)
    for tap_f in range(3):
        for tap_h in range(3):
            for tap_w in range(3):
                index = (tap_f * 3 + tap_h) * 3 + tap_w
                behind = tap_block(
                    padded_grad, 2 - tap_f, 2 - tap_h, 2 - tap_w, frame_count, row_count, col_count
                )
                partial_flat = partial_flat + lax.dot_general(
                    behind,
                    kernel[index],
                    (((1,), (1,)), ((), ())),
                    preferred_element_type=jnp.float32,
                )
    partial_input = partial_flat.reshape(frame_count, row_count, col_count, chan_count)
    grad_hidden = lax.psum(partial_input, "seq")
    grad_features = (silu_grad(inner_vals) * grad_hidden * frame_mask).astype(jnp.bfloat16)
    return (pose_tokens[None], grad_features[None], grad_weight, grad_bias)


def solution(mesh):
    return jax.shard_map(
        shards,
        mesh=mesh,
        in_specs=(
            P("dp", None, "tile", None, None),
            P("dp"),
            P(("dp", "tile"), "seq"),
            P("seq"),
            P("dp", "seq", "tile", None, None),
        ),
        out_specs=(
            P("dp", "seq", "tile", None, None),
            P("dp", None, "tile", None, None),
            P(("dp", "tile"), "seq"),
            P("seq"),
        ),
        check_vma=False,
    )
```

profile of v0, /device:TPU:1, one launch (start us, length us, event | category | flops | bytes accessed | tf_op | source)
XLA Modules:
  0.0 874.1 jit_solution(13256543171585304704)
XLA Ops:
  7.9 25.1 %copy.20 = bf16[1,4,4,32,5120]{3,2,1,4,0:T(4,128)(2,1)} copy(bf16[1,4,4,32,5120]{4,3,2,1,0:T(8,128)(2,1)} %param.9) | data formatting | bytes 10485760 | tf_op args[4]
  33.0 15.5 %bitcast_bitcast_fusion = bf16[5120,4,4,32]{3,2,1,0:T(4,128)(2,1)} fusion(bf16[1,4,4,32,5120]{3,2,1,4,0:T(4,128)(2,1)} %copy.20), kind=kLoop, calls=%fused_computation.295 | loop fusion | bytes 10485760
  48.4 30.8 %reshape.369 = bf16[2,2,655360]{2,1,0:T(2,128)(2,1)} reshape(bf16[5120,4,4,32]{3,2,1,0:T(4,128)(2,1)} %bitcast_bitcast_fusion) | data formatting | bytes 10485760
  79.2 6.0 all-to-all-start.1
  86.2 57.8 %all-to-all-done.1 = bf16[2,2,655360]{2,1,0:T(2,128)(2,1)} async-done(((bf16[2,2,655360]{2,1,0:T(2,128)(2,1)}), bf16[2,2,655360]{2,1,0:T(2,128)(2,1)}, u32[]{:S(2)}, u32[]{:S(2)}) %all-to-all-start.1) | async-done | bytes 5242912 | tf_op jit(solution)/shard_map/all_to_all | solution.py:62
  144.0 22.1 %reshape.370 = bf16[5120,4,4,32]{3,2,1,0:T(4,128)(2,1)} reshape(bf16[2,2,655360]{2,1,0:T(2,128)(2,1)} %all-to-all-done.1) | data formatting | bytes 10485760
  166.1 31.2 %copy.52 = bf16[4,4,32,2,2560]{4,3,2,1,0:T(2,128)(2,1)} copy(bf16[4,4,32,2,2560]{2,1,0,4,3:T(4,128)(2,1)} %bitcast.378) | data formatting | bytes 10485760 | tf_op jit(solution)/shard_map/all_to_all | solution.py:62
  218.6 7.3 collective-permute-done.2
  230.3 5.6 pad_maximum_fusion.1
  235.9 11.6 %select_maximum_fusion = bf16[10,6,34,2560]{3,2,1,0:T(8,128)(2,1)S(1)} fusion(bf16[8,1,32,2560]{3,2,1,0:T(8,128)(2,1)} %collective-permute-done.3, bf16[8,4,32,2560]{3,2,1,0:T(8,128)(2,1)S(1)} %bitcast.375, bf16[8,1,32,2560]{3,2,1,0:T(8,128)(2,1)S(1)} %collective-permute-done.2), kind=kLoop, calls=%fused_computation.7 | loop fusion | flops 99225600 | bytes 18309120 | tf_op jit(solution)/shard_map/concatenate | solution.py:16
  252.0 9.3 %fusion.231 = (bf16[8,4,32,2560]{3,2,1,0:T(8,128)(2,1)}, bf16[8,4,32,2560]{3,2,1,0:T(8,128)(2,1)}, bf16[8,4,32,2560]{3,2,1,0:T(8,128)(2,1)}, bf16[8,4,32,2560]{3,2,1,0:T(8,128)(2,1)}, bf16[8,4,32,2560]{3,2,1,0:T(8,128)(2,1)}) fusion(bf16[10,6,34,2560]{3,2,1,0:T(8,128)(2,1)S(1)} %select_maximum_fusion), kind=kLoop, calls=%fused_computation.290 | loop fusion | bytes 52428800 | tf_op jit(solution)/shard_map/slice | solution.py:26
  261.4 79.6 %fusion.230 = (bf16[8,4,32,2560]{3,2,1,0:T(8,128)(2,1)}, bf16[8,4,32,2560]{3,2,1,0:T(8,128)(2,1)}, bf16[8,4,32,2560]{3,2,1,0:T(8,128)(2,1)}, bf16[8,4,32,2560]{3...) fusion(bf16[10,6,34,2560]{3,2,1,0:T(8,128)(2,1)} %copy-done.1), kind=kLoop, calls=%fused_computation.289 | loop fusion | bytes 199229440 | tf_op jit(solution)/shard_map/slice | solution.py:26
  373.4 5.5 fusion.125
  415.7 27.4 %all-reduce.4.cloned.1.call-done = f32[8,4,32,128]{3,2,1,0:T(8,128)} async-done(((f32[8,4,32,128]{3,2,1,0:T(8,128)}), f32[8,4,32,128]{3,2,1,0:T(8,128)}) %all-reduce.4.cloned.1.call-update) | async-done | bytes 524304 | tf_op jit(solution)/shard_map/psum | solution.py:101
  451.0 11.3 %convert_reduce_fusion = (f32[2560]{0:T(1024)}, bf16[2,4,4,32,2560]{4,0,3,2,1:T(2,128)(2,1)S(1)}) fusion(bf16[2,4]{0,1:T(4,128)(2,1)S(1)} %convert_convert_fusion, bf16[4,4,32,2,2560]{4,3,2,1,0:T(2,128)(2,1)} %copy.52), kind=kLoop, calls=%fused_computation.12 | loop fusion | flops 7861760 | bytes 10496016 | tf_op jit(solution)/shard_map/reduce_sum | solution.py:81
  518.4 7.9 fusion.115
  527.8 10.1 %fusion.127 = f32[1024,2560]{1,0:T(8,128)} fusion(bf16[1024,128]{1,0:T(8,128)(2,1)S(1)} %bitcast.467, bf16[3456,2560]{1,0:T(8,128)(2,1)} %all-gather.2.cloned.1.call-done), kind=kOutput, calls=%fused_computation.177 | convolution fusion | flops 671088640 | bytes 11403264 | tf_op jit(solution)/shard_map/dot_general | solution.py:54
  537.9 7.2 fusion.101
  545.2 7.2 fusion.108
  552.4 7.3 fusion.111
  559.7 7.0 fusion.119
  572.1 5.6 fusion.131
  583.2 5.8 fusion.139
  632.7 5.6 fusion.89
  660.0 5.5 fusion.159
  676.4 88.7 %add_add_fusion = f32[1024,2560]{1,0:T(8,128)} fusion(f32[1024,2560]{1,0:T(8,128)} %fusion.65, f32[1024,2560]{1,0:T(8,128)} %fusion.69, f32[1024,2560]{1,0:T(8,128)} %fusion.73, f32[1024,2560]{1,0:T(8,128)} %fusion.77, f32[1024,2560]{1,0:T(8,128)} %fusion.81, f32[1024,2560]{1,0:T(8,128)} %fusion.85, f32[1024,2560]{1,0:T(8,128)} %fusion.89, ...), kind=kOutput, calls=%fused_computation.14 | convolution fusion | flops 739246080 | bytes 284033024 | tf_op jit(solution)/shard_map/dot_general | solution.py:54
  765.1 8.4 multiply_convert_fusion
  773.6 5.9 all-to-all-start
  779.5 57.9 %psum.15 = f32[2560]{0:T(1024)} all-reduce(f32[2560]{0:T(1024)S(1)} %copy-done.21), channel_id=1, replica_groups=mesh['dp'=4,'tile'=4,'seq'=2] {'dp','tile'}, use_global_device_ids=true, to_apply=%region_3.4 | all-reduce | flops 2560 | bytes 20480 | tf_op jit(solution)/shard_map/psum | solution.py:83
  837.4 10.3 %copy.54 = bf16[2,4,4,32,2560]{4,0,3,2,1:T(2,128)(2,1)} copy(bf16[2,4,4,32,2560]{4,3,2,1,0:T(8,128)(2,1)} %bitcast.30) | data formatting | bytes 10485760 | tf_op jit(solution)/shard_map/all_to_all | solution.py:61
  847.8 12.4 %broadcast_in_dim.8 = bf16[1,4,4,32,5120]{4,3,2,1,0:T(8,128)(2,1)} reshape(bf16[4,4,32,2,2560]{4,3,2,1,0:T(2,128)(2,1)} %bitcast.388) | data formatting | bytes 10485760 | tf_op jit(solution)/shard_map/broadcast_in_dim | solution.py:103
  860.1 7.2 reduce-scatter.2.cloned.1.call-done
  (282 shorter events, 252.3 us)
Async XLA Ops:
  7.2 333.9 %all-gather.2.cloned.1.call-start = ((), (), s32[]{:S(2)}) async-start(), calls=%async_computation.3 | async-start | bytes 18800640 | tf_op jit(solution)/shard_map/all_gather | solution.py:41
  79.2 64.8 %all-to-all-start.1 = ((bf16[2,2,655360]{2,1,0:T(2,128)(2,1)}), bf16[2,2,655360]{2,1,0:T(2,128)(2,1)}, u32[]{:S(2)}, u32[]{:S(2)}) async-start(bf16[2,2,655360]{2,1,0:T(2,128)(2,1)} %reshape.369), calls=%async_computation.1 | async-start | bytes 10485760 | tf_op jit(solution)/shard_map/all_to_all | solution.py:62
  85.3 357.8 %all-reduce.4.cloned.1.call-start = ((), (), s32[]{:S(2)}) async-start(), calls=%async_computation.4 | async-start | bytes 1048576 | tf_op jit(solution)/shard_map/psum | solution.py:101
  206.1 24.2 %slice-start = ((s8[5242880]{0:T(1024)(128)(4,1)}), s8[1048576]{0:T(1024)(128)(4,1)S(1)}, s32[]{:S(2)}) async-start(s8[5242880]{0:T(1024)(128)(4,1)} %bitcast.374), calls=%async_computation.6 | async-start | bytes 2097152
  206.1 19.8 %collective-permute-start.2 = (bf16[8,1,32,2560]{3,2,1,0:T(8,128)(2,1)}, bf16[8,1,32,2560]{3,2,1,0:T(8,128)(2,1)S(1)}, u32[]{:S(2)}, u32[]{:S(2)}) collective-permute-start(bf16[8,1,32,2560]{3,2,1,0:T(8,128)(2,1)} %get-tuple-element.32), channel_id=1, source_target_pairs={{0,2},{2,4},{4,6},{1,3},{3,5},{5,7},{8,10},{10,12},{12,14},{9,11},... | collective-permute-start | bytes 3932168 | tf_op jit(solution)/shard_map/ppermute | solution.py:12
  211.1 19.2 %collective-permute-start.3 = (bf16[8,1,32,2560]{3,2,1,0:T(8,128)(2,1)}, bf16[8,1,32,2560]{3,2,1,0:T(8,128)(2,1)}, u32[]{:S(2)}, u32[]{:S(2)}) collective-permute-start(bf16[8,1,32,2560]{3,2,1,0:T(8,128)(2,1)} %get-tuple-element.33), channel_id=1, source_target_pairs={{2,0},{4,2},{6,4},{3,1},{5,3},{7,5},{10,8},{12,10},{14,12},{11,9},... | collective-permute-start | bytes 3932168 | tf_op jit(solution)/shard_map/ppermute | solution.py:15
  213.2 17.2 %slice-start.1 = ((s8[5242880]{0:T(1024)(128)(4,1)}), s8[4194304]{0:T(1024)(128)(4,1)S(1)}, s32[]{:S(2)}) async-start(s8[5242880]{0:T(1024)(128)(4,1)} %bitcast.374), calls=%async_computation.7 | async-start | bytes 8388608
  341.0 14.2 %copy-start.3 = (bf16[3456,2560]{1,0:T(8,128)(2,1)S(1)}, bf16[3456,2560]{1,0:T(8,128)(2,1)}, u32[]{:S(2)}) copy-start(bf16[3456,2560]{1,0:T(8,128)(2,1)} %all-gather.2.cloned.1.call-done) | copy-start | bytes 53084164
  345.3 14.1 %copy-start.4 = (bf16[8,4,32,2560]{3,2,1,0:T(8,128)(2,1)S(1)}, bf16[8,4,32,2560]{3,2,1,0:T(8,128)(2,1)}, u32[]{:S(2)}) copy-start(bf16[8,4,32,2560]{3,2,1,0:T(8,128)(2,1)} %get-tuple-element.21) | copy-start | bytes 15728644
  350.3 10.6 %slice-start.37 = ((s8[5242880]{0:T(1024)(128)(4,1)}), s8[4194304]{0:T(1024)(128)(4,1)S(1)}, s32[]{:S(2)}) async-start(s8[5242880]{0:T(1024)(128)(4,1)} %bitcast.427), calls=%async_computation.43 | async-start | bytes 8388608
  355.2 8.1 slice-start.35
  370.3 8.7 slice-start.47
  371.8 9.5 %slice-start.31 = ((s8[5242880]{0:T(1024)(128)(4,1)}), s8[4194304]{0:T(1024)(128)(4,1)S(1)}, s32[]{:S(2)}) async-start(s8[5242880]{0:T(1024)(128)(4,1)} %bitcast.418), calls=%async_computation.37 | async-start | bytes 8388608
  373.4 9.5 %slice-start.29 = ((s8[5242880]{0:T(1024)(128)(4,1)}), s8[4194304]{0:T(1024)(128)(4,1)S(1)}, s32[]{:S(2)}) async-start(s8[5242880]{0:T(1024)(128)(4,1)} %bitcast.415), calls=%async_computation.35 | async-start | bytes 8388608
  373.4 7.9 slice-start.32
  384.5 7.3 slice-start.21
  386.8 7.3 slice-start.19
  409.9 33.1 %copy-start.5 = (bf16[1,8,4,32,128]{4,3,2,1,0:T(8,128)(2,1)S(1)}, bf16[1,8,4,32,128]{4,3,2,1,0:T(8,128)(2,1)}, u32[]{:S(2)}) copy-start(bf16[1,8,4,32,128]{4,3,2,1,0:T(8,128)(2,1)} %param.5) | copy-start | bytes 786436
  415.6 451.8 %reduce-scatter.2.cloned.1.call-start = ((), (), s32[]{:S(2)}) async-start(), calls=%async_computation.5 | async-start | bytes 37601280 | tf_op jit(solution)/shard_map/reduce_scatter | solution.py:82
  415.7 101.3 %copy-start.23 = (f32[8]{0:T(128)}, f32[8]{0:T(128)S(1)}, u32[]{:S(2)}) copy-start(f32[8]{0:T(128)S(1)} %compare_convert_fusion) | copy-start | bytes 100
  445.1 18.3 %collective-permute-start = (bf16[8,1,32,128]{3,2,1,0:T(8,128)(2,1)S(1)}, bf16[8,1,32,128]{3,2,1,0:T(8,128)(2,1)S(1)}, u32[]{:S(2)}, u32[]{:S(2)}) collective-permute-start(bf16[8,1,32,128]{3,2,1,0:T(8,128)(2,1)S(1)} %get-tuple-element.62), channel_id=1, source_target_pairs={{0,2},{2,4},{4,6},{1,3},{3,5},{5,7},{8,10},{10,12},{12,14},{9,11},... | collective-permute-start | bytes 196616 | tf_op jit(solution)/shard_map/ppermute | solution.py:12
  448.8 14.9 %slice-start.2 = ((s8[5242880]{0:T(1024)(128)(4,1)}), s8[4194304]{0:T(1024)(128)(4,1)S(1)}, s32[]{:S(2)}) async-start(s8[5242880]{0:T(1024)(128)(4,1)} %bitcast.376), calls=%async_computation.8 | async-start | bytes 8388608
  448.8 14.7 %collective-permute-start.1 = (bf16[8,1,32,128]{3,2,1,0:T(8,128)(2,1)S(1)}, bf16[8,1,32,128]{3,2,1,0:T(8,128)(2,1)S(1)}, u32[]{:S(2)}, u32[]{:S(2)}) collective-permute-start(bf16[8,1,32,128]{3,2,1,0:T(8,128)(2,1)S(1)} %get-tuple-element.63), channel_id=1, source_target_pairs={{2,0},{4,2},{6,4},{3,1},{5,3},{7,5},{10,8},{12,10},{14,12},{11,9},... | collective-permute-start | bytes 196616 | tf_op jit(solution)/shard_map/ppermute | solution.py:15
  518.4 19.5 %slice-start.8 = ((s8[17694720]{0:T(1024)(128)(4,1)}), s8[917504]{0:T(1024)(128)(4,1)S(1)}, s32[]{:S(2)}) async-start(s8[17694720]{0:T(1024)(128)(4,1)} %bitcast.389), calls=%async_computation.14 | async-start | bytes 1835008
  518.4 19.5 %slice-start.9 = ((s8[17694720]{0:T(1024)(128)(4,1)}), s8[4194304]{0:T(1024)(128)(4,1)S(1)}, s32[]{:S(2)}) async-start(s8[17694720]{0:T(1024)(128)(4,1)} %bitcast.389), calls=%async_computation.15 | async-start | bytes 8388608
  526.3 11.6 %slice-start.10 = ((s8[17694720]{0:T(1024)(128)(4,1)}), s8[4194304]{0:T(1024)(128)(4,1)S(1)}, s32[]{:S(2)}) async-start(s8[17694720]{0:T(1024)(128)(4,1)} %bitcast.389), calls=%async_computation.16 | async-start | bytes 8388608
  526.6 11.3 %slice-start.11 = ((s8[17694720]{0:T(1024)(128)(4,1)}), s8[4194304]{0:T(1024)(128)(4,1)S(1)}, s32[]{:S(2)}) async-start(s8[17694720]{0:T(1024)(128)(4,1)} %bitcast.389), calls=%async_computation.17 | async-start | bytes 8388608
  527.8 10.1 %slice-start.12 = ((s8[17694720]{0:T(1024)(128)(4,1)}), s8[4194304]{0:T(1024)(128)(4,1)S(1)}, s32[]{:S(2)}) async-start(s8[17694720]{0:T(1024)(128)(4,1)} %bitcast.389), calls=%async_computation.18 | async-start | bytes 8388608
  676.4 88.7 %copy-start.22 = (f32[2560]{0:T(1024)S(1)}, f32[2560]{0:T(1024)}, u32[]{:S(2)}) copy-start(f32[2560]{0:T(1024)} %convert_element_type.74) | copy-start | bytes 30724
  676.4 88.7 %copy-start.24 = (f32[8]{0:T(128)S(1)}, f32[8]{0:T(128)}, u32[]{:S(2)}) copy-start(f32[8]{0:T(128)} %copy-done.23) | copy-start | bytes 100
  765.1 14.4 %copy-start.21 = (f32[2560]{0:T(1024)S(1)}, f32[2560]{0:T(1024)}, u32[]{:S(2)}) copy-start(f32[2560]{0:T(1024)} %get-tuple-element.4) | copy-start | bytes 30724
  773.6 63.9 %all-to-all-start = ((bf16[8,4,32,2560]{3,2,1,0:T(8,128)(2,1)}), bf16[8,4,32,2560]{3,2,1,0:T(8,128)(2,1)}, u32[]{:S(2)}, u32[]{:S(2)}) async-start(bf16[8,4,32,2560]{3,2,1,0:T(8,128)(2,1)} %multiply_convert_fusion), calls=%async_computation | async-start | bytes 10485760 | tf_op jit(solution)/shard_map/all_to_all | solution.py:61
  (54 other events, 264.1 us)
Sparse Core Ops, SparseCore 0:
  9.6 95.8 all-gather.1
  415.7 27.2 all-reduce.3
  517.0 350.2 reduce-scatter.1
where the time goes:
time: 881 us; the launch traced here: 874 us
  matrix products  370 us (42%)
  local copies, waits for them, and re-layouts  255 us (29%)
  waiting for transfers between devices  105 us (12%)
  blocking collectives  57.9 us (7%)
  other arithmetic  46.2 us (5%)
  starting transfers between devices  25 us (3%)
  between operations  15.6 us (2%)
    dot_general x27, matrix products, shards(): jnp.dot(columns, kernel[index], preferred_element_type=jnp.float32)  245 us
    unnamed x158, local copies, waits for them, and re-layouts  103 us
    slice x4, local copies, waits for them, and re-layouts, tap_block(): padded[start_f:start_f + frame_count, start_h:start_h + row_count, start_...  90.4 us
    dot_general x27, matrix products, shards(): lax.dot_general(behind, kernel[index], (((1,), (1,)), ((), ())), preferre...  71.6 us
    psum x1, blocking collectives, shards(): grad_bias = lax.psum(bias_term, ('dp', 'tile'))  57.9 us
    all_to_all x1, waiting for transfers between devices, shards(): lax.all_to_all(cotangent[0], 'seq', split_axis=3, concat_axis=0, tiled=True)  57.8 us
    dot_general x27, matrix products, shards(): lax.dot_general(columns, flat_grad, (((0,), (0,)), ((), ())), preferred_e...  53.2 us
    all_to_all x2, local copies, waits for them, and re-layouts, shards(): lax.all_to_all(cotangent[0], 'seq', split_axis=3, concat_axis=0, tiled=True)  34.8 us
  transfers between devices with their start and end apart: 9, of which 5 were waited for; matrix products, arithmetic and copies ran while one was open for 61% of the time, Pallas kernels for 0%

commit v1 on v0

v1 whole, which is shorter than its diff:
```python
import jax
import jax.numpy as jnp
from jax import lax
from jax.sharding import PartitionSpec as P


def pick(pieces, index):
    result = pieces[0]
    for place in range(1, len(pieces)):
        result = jnp.where(index == place, pieces[place], result)
    return result


def swap(value, axis, distance):
    count = lax.axis_size(axis)
    return lax.ppermute(value, axis, [(i, i ^ distance) for i in range(count)])


def sum_over(value, axes):
    for axis in axes:
        distance = 1
        while distance < lax.axis_size(axis):
            value = value + swap(value, axis, distance)
            distance *= 2
    return value


def exchange(parts, axis):
    me = lax.axis_index(axis)
    count = lax.axis_size(axis)
    by_offset = [pick(parts, me)]
    for offset in range(1, count):
        by_offset.append(swap(pick(parts, me ^ offset), axis, offset))
    return [pick(by_offset, me ^ source) for source in range(count)]


def neighbours(low_row, high_row, axis):
    count = lax.axis_size(axis)
    forward = [(i, i + 1) for i in range(count - 1)]
    backward = [(i + 1, i) for i in range(count - 1)]
    return lax.ppermute(high_row, axis, forward), lax.ppermute(low_row, axis, backward)


def silu_grad(values):
    sigma = jax.nn.sigmoid(values)
    return sigma * (1.0 + values * (1.0 - sigma))


def shards(features, lengths, weight, bias, cotangent):
    seq_count = lax.axis_size("seq")
    local_feat = features[0]
    frame_count, row_count, col_count, chan_count = local_feat.shape
    row_total = frame_count * row_count * col_count
    share = weight.shape[1]
    frame_share = frame_count // seq_count
    frame_mask = (jnp.arange(frame_count) < lengths[0]).astype(jnp.float32)[:, None, None, None]

    cot = cotangent[0]
    received = exchange(
        [cot[..., j * share : (j + 1) * share] for j in range(seq_count)], "seq"
    )
    grad_out = jnp.concatenate(received, axis=0) * frame_mask.astype(jnp.bfloat16)
    flat_grad = grad_out.reshape(row_total, share)

    inner_vals = local_feat.astype(jnp.float32)
    hidden = (jax.nn.silu(inner_vals) * frame_mask).astype(jnp.bfloat16)
    above, below = neighbours(hidden[:, :1], hidden[:, -1:], "tile")
    padded = jnp.pad(
        jnp.concatenate([above, hidden, below], axis=1), ((1, 1), (0, 0), (1, 1), (0, 0))
    )
    wide = jnp.concatenate([padded[:, :, e : e + col_count] for e in range(3)], axis=3)
    columns = jnp.concatenate(
        [wide[a : a + frame_count, b : b + row_count] for a in range(3) for b in range(3)], axis=3
    ).reshape(row_total, 27 * chan_count)

    weight_term = lax.dot_general(
        columns, flat_grad, (((0,), (0,)), ((), ())), preferred_element_type=jnp.float32
    ).astype(jnp.bfloat16)
    grad_weight = lax.psum_scatter(
        weight_term, ("dp", "tile"), scatter_dimension=0, tiled=True
    ).astype(jnp.float32)
    grad_bias = sum_over(jnp.sum(flat_grad, axis=0, dtype=jnp.float32), ("tile", "dp"))

    full_weight = lax.all_gather(weight, ("dp", "tile"), axis=0, tiled=True)
    output = jnp.dot(columns, full_weight, preferred_element_type=jnp.float32)
    tokens = (
        (output.reshape(frame_count, row_count, col_count, share) + bias.astype(jnp.float32))
        * frame_mask
    ).astype(jnp.bfloat16)
    pose_tokens = jnp.concatenate(
        exchange(
            [tokens[j * frame_share : (j + 1) * frame_share] for j in range(seq_count)], "seq"
        ),
        axis=3,
    )

    spread = lax.dot_general(
        flat_grad, full_weight, (((1,), (1,)), ((), ())), preferred_element_type=jnp.float32
    ).reshape(frame_count, row_count, col_count, 27 * chan_count)
    total = jnp.zeros((frame_count, row_count + 2, col_count, chan_count), jnp.float32)
    for a in range(3):
        for b in range(3):
            start = (a * 3 + b) * 3 * chan_count
            first = spread[..., start : start + chan_count]
            second = spread[..., start + chan_count : start + 2 * chan_count]
            third = spread[..., start + 2 * chan_count : start + 3 * chan_count]
            none = ((0, 0), (0, 0))
            joined = (
                jnp.pad(first[:, :, 1:], (*none, (0, 1), (0, 0)))
                + second
                + jnp.pad(third[:, :, :-1], (*none, (1, 0), (0, 0)))
            )
            kept = joined[max(0, 1 - a) : frame_count - max(0, a - 1)]
            total = total + jnp.pad(
                kept, ((max(0, a - 1), max(0, 1 - a)), (b, 2 - b), (0, 0), (0, 0))
            )
    from_above, from_below = neighbours(total[:, :1], total[:, -1:], "tile")
    rims = jnp.concatenate(
        [from_above, jnp.zeros_like(total[:, 2:-2]), from_below], axis=1
    )
    grad_hidden = sum_over(total[:, 1:-1] + rims, ("seq",))
    grad_features = (silu_grad(inner_vals) * grad_hidden * frame_mask).astype(jnp.bfloat16)
    return (pose_tokens[None], grad_features[None], grad_weight, grad_bias)


def solution(mesh):
    return jax.shard_map(
        shards,
        mesh=mesh,
        in_specs=(
            P("dp", None, "tile", None, None),
            P("dp"),
            P(("dp", "tile"), "seq"),
            P("seq"),
            P("dp", "seq", "tile", None, None),
        ),
        out_specs=(
            P("dp", "seq", "tile", None, None),
            P("dp", None, "tile", None, None),
            P(("dp", "tile"), "seq"),
            P("seq"),
        ),
        check_vma=False,
    )
```

time: 881 us -> 396 us (0.45)
  matrix products: 370 us -> 72 us
  local copies, waits for them, and re-layouts: 255 us -> 10.9 us
  waiting for transfers between devices: 105 us -> 253 us
  blocking collectives: 57.9 us -> 0 us
  other arithmetic: 46.2 us -> 23.3 us
    dot_general x54 -> x2, matrix products: 317 us -> 50.5 us  [the longest x1 26.6 us: shards(): lax.dot_general(flat_grad, full_weight, (((1,), (1,)), ((), ())), preferr...]
    ppermute x4 -> x11, waiting for transfers between devices: 11.7 us -> 118 us  [the longest x7 115 us: swap(): return lax.ppermute(value, axis, [(i, i ^ distance) for i in range(count)])]
    unnamed x158 -> x22, local copies, waits for them, and re-layouts: 103 us -> 5.3 us
    reduce_scatter x1, waiting for transfers between devices: 7.25 us -> 103 us  [shards(): lax.psum_scatter(weight_term, ('dp', 'tile'), scatter_dimension=0, tiled=...]
    slice x6 -> x4, local copies, waits for them, and re-layouts: 92.2 us -> 5.42 us  [the longest x1 5.08 us: shards(): first[:, :, 1:]]
    psum x1 -> x0, blocking collectives: 57.9 us -> none  [shards(): grad_bias = lax.psum(bias_term, ('dp', 'tile'))]
    all_to_all x2 -> x0, waiting for transfers between devices: 57.8 us -> none  [the longest x1 57.8 us: shards(): lax.all_to_all(cotangent[0], 'seq', split_axis=3, concat_axis=0, tiled=True)]
    all_to_all x3 -> x0, local copies, waits for them, and re-layouts: 45.1 us -> none  [the longest x2 34.8 us: shards(): lax.all_to_all(cotangent[0], 'seq', split_axis=3, concat_axis=0, tiled=True)]
  transfers between devices with their start and end apart: 9 -> 13, of which waited for: 5 -> 12; matrix products, arithmetic and copies ran while one was open for 61% -> 10% of each run, Pallas kernels for 0% -> 0%
where the time goes in v1:
time: 396 us
  waiting for transfers between devices  253 us (64%)
  matrix products  72 us (18%)
  other arithmetic  23.3 us (6%)
  starting transfers between devices  21.6 us (5%)
  between operations  15 us (4%)
  local copies, waits for them, and re-layouts  10.9 us (3%)
    ppermute x7, waiting for transfers between devices, swap(): return lax.ppermute(value, axis, [(i, i ^ distance) for i in range(count)])  115 us
    reduce_scatter x1, waiting for transfers between devices, shards(): lax.psum_scatter(weight_term, ('dp', 'tile'), scatter_dimension=0, tiled=...  103 us
    all_gather x1, waiting for transfers between devices, shards(): full_weight = lax.all_gather(weight, ('dp', 'tile'), axis=0, tiled=True)  30.9 us
    dot_general x1, matrix products, shards(): lax.dot_general(flat_grad, full_weight, (((1,), (1,)), ((), ())), preferr...  26.6 us
    dot_general x1, matrix products, shards(): output = jnp.dot(columns, full_weight, preferred_element_type=jnp.float32)  23.9 us
    dot_general x1, matrix products, shards(): lax.dot_general(columns, flat_grad, (((0,), (0,)), ((), ())), preferred_e...  21.5 us
    ppermute x7, starting transfers between devices, swap(): return lax.ppermute(value, axis, [(i, i ^ distance) for i in range(count)])  10.2 us
    select_n x4, other arithmetic, pick(): result = jnp.where(index == place, pieces[place], result)  8.58 us
  transfers between devices with their start and end apart: 13, of which 12 were waited for; matrix products, arithmetic and copies ran while one was open for 10% of the time, Pallas kernels for 0%

profile of v1, /device:TPU:1, one launch (start us, length us, event | category | flops | bytes accessed | tf_op | source)
XLA Modules:
  0.0 395.6 jit_solution(2411242803760982149)
XLA Ops:
  8.0 2.8 broadcast_select_fusion.1
  10.8 2.1 collective-permute-start.3
  13.6 56.0 %collective-permute-done.3 = bf16[4,4,32,2560]{3,2,1,0:T(8,128)(2,1)} collective-permute-done((bf16[4,4,32,2560]{3,2,1,0:T(8,128)(2,1)S(1)}, bf16[4,4,32,2560]{3,2,1,0:T(8,128)(2,1)}, u32[]{:S(2)}, u32[]{:S(2)}) %collective-permute-start.3) | collective-permute-done | bytes 2621472 | tf_op jit(solution)/shard_map/ppermute | solution.py:16
  69.6 5.0 %broadcast_select_fusion.4 = (bf16[4,4,32,2560]{3,2,1,0:T(8,128)(2,1)S(1)}, bf16[4,4,32,2560]{3,2,1,0:T(8,128)(2,1)}) fusion(bf16[4,4,32,2560]{3,2,1,0:T(8,128)(2,1)} %collective-permute-done.3, pred[]{:T(512)S(6)} %eq.4, bf16[4,4,32,5120]{3,2,1,0:T(8,128)(2,1)} %bitcast.30, pred[]{:T(512)S(6)} %eq.5), kind=kLoop, calls=%fused_computation.13 | loop fusion | flops 3932160 | bytes 13107202 | tf_op jit(solution)/shard_map/jit(_where)/select_n | solution.py:10
  74.6 30.9 %all-gather.2.cloned.1.call-done = bf16[3456,2560]{1,0:T(8,128)(2,1)} async-done(((bf16[216,2560]{1,0:T(8,128)(2,1)}), bf16[3456,2560]{1,0:T(8,128)(2,1)}) %all-gather.2.cloned.1.call-update) | async-done | bytes 17694736 | tf_op jit(solution)/shard_map/all_gather | solution.py:84
  105.5 26.6 %fusion = f32[8,4,32,3456]{3,2,1,0:T(8,128)} fusion(bf16[3456,2560]{1,0:T(8,128)(2,1)} %all-gather.2.cloned.1.call-done, bf16[4,4,32,2560]{3,2,1,0:T(8,128)(2,1)} %get-tuple-element.32, bf16[4,4,32,2560]{3,2,1,0:T(8,128)(2,1)S(1)} %get-tuple-element.31, bf16[8]{0:T(256)(128)(2,1)S(1)} %fusion.26), kind=kOutput, calls=%fused_computation.1 | convolution fusion | flops 18124636160 | bytes 37093392 | tf_op jit(solution)/shard_map/dot_general | solution.py:97
  132.1 5.1 %fusion.27 = (f32[8,4,31,128]{3,2,1,0:T(8,128)S(1)}, f32[8,4,31,128]{3,2,1,0:T(8,128)S(1)}, f32[8,4,31,128]{3,2,1,0:T(8,128)S(1)}, f32[8,4,31,128]{3,2,1,0:T(8,1...) fusion(f32[8,4,32,3456]{3,2,1,0:T(8,128)} %fusion), kind=kLoop, calls=%fused_computation.75 | loop fusion | bytes 18284544 | tf_op jit(solution)/shard_map/slice | solution.py:109
  137.2 3.5 fusion.28
  142.3 2.1 collective-permute-start.5
  144.5 3.4 collective-permute-start.4
  148.6 1.2 collective-permute-done.4
  150.0 1.2 collective-permute-start.6
  151.2 11.0 %collective-permute-done.6 = f32[8,4,32,128]{3,2,1,0:T(8,128)S(1)} collective-permute-done((f32[8,4,32,128]{3,2,1,0:T(8,128)S(1)}, f32[8,4,32,128]{3,2,1,0:T(8,128)S(1)}, u32[]{:S(2)}, u32[]{:S(2)}) %collective-permute-start.6) | collective-permute-done | bytes 524320 | tf_op jit(solution)/shard_map/ppermute | solution.py:16
  163.2 1.9 collective-permute-start.1
  165.2 3.8 collective-permute-start
  169.0 1.1 collective-permute-done
  172.2 2.9 copy-done.3
  175.1 21.5 %bitcast_convert_fusion = bf16[3456,2560]{1,0:T(8,128)(2,1)} fusion(bf16[8,4,32,3456]{3,2,1,0:T(8,128)(2,1)S(1)} %slice_dynamic-update-slice_fusion, bf16[4,4,32,2560]{3,2,1,0:T(8,128)(2,1)S(1)} %copy-done, bf16[4,4,32,2560]{3,2,1,0:T(8,128)(2,1)S(1)} %get-tuple-element.31, bf16[8]{0:T(256)(128)(2,1)S(1)} %fusion.26), kind=kOutput, calls=%fused_computation | convolution fusion | flops 18133483520 | bytes 30015504 | tf_op jit(solution)/shard_map/dot_general | solution.py:76
  197.3 23.9 %multiply_convert_fusion = bf16[8,4,32,2560]{3,2,1,0:T(8,128)(2,1)S(1)} fusion(bf16[8,4,32,3456]{3,2,1,0:T(8,128)(2,1)} %copy-done.3, bf16[3456,2560]{1,0:T(8,128)(2,1)} %all-gather.2.cloned.1.call-done, f32[8]{0:T(128)S(1)} %copy-done.6, f32[2560]{0:T(1024)S(1)} %convert_element_type.90), kind=kOutput, calls=%fused_computation.6 | convolution fusion | flops 18127257600 | bytes 30025760 | tf_op jit(solution)/shard_map/dot_general | solution.py:85
  221.5 1.3 collective-permute-start.2
  223.4 1.5 convert_reduce_fusion
  225.1 1.2 collective-permute-done.7
  226.2 2.1 collective-permute-start.8
  228.3 1.4 collective-permute-done.8
  229.7 1.2 collective-permute-start.9
  230.9 1.6 collective-permute-done.9
  232.6 2.1 collective-permute-start.10
  234.7 1.3 collective-permute-done.10
  236.6 42.8 %collective-permute-done.2 = bf16[4,4,32,2560]{3,2,1,0:T(8,128)(2,1)S(1)} collective-permute-done((bf16[4,4,32,2560]{3,2,1,0:T(8,128)(2,1)S(1)}, bf16[4,4,32,2560]{3,2,1,0:T(8,128)(2,1)S(1)}, u32[]{:S(2)}, u32[]{:S(2)}) %collective-permute-start.2) | collective-permute-done | bytes 2621472 | tf_op jit(solution)/shard_map/ppermute | solution.py:16
  279.9 3.0 maximum_bitcast_fusion
  282.9 103.0 %reduce-scatter.2.cloned.1.call-done = bf16[216,2560]{1,0:T(8,128)(2,1)} async-done(((bf16[3456,2560]{1,0:T(8,128)(2,1)}), bf16[216,2560]{1,0:T(8,128)(2,1)}) %reduce-scatter.2.cloned.1.call-update) | async-done | bytes 1105936 | tf_op jit(solution)/shard_map/reduce_scatter | solution.py:79
  385.9 2.9 convert_element_type.95
  (51 shorter events, 9.0 us)
Async XLA Ops:
  7.2 98.4 %all-gather.2.cloned.1.call-start = ((), (), s32[]{:S(2)}) async-start(), calls=%async_computation.1 | async-start | bytes 18800640 | tf_op jit(solution)/shard_map/all_gather | solution.py:84
  7.9 378.0 %reduce-scatter.2.cloned.1.call-start = ((), (), s32[]{:S(2)}) async-start(), calls=%async_computation.2 | async-start | bytes 18800640 | tf_op jit(solution)/shard_map/reduce_scatter | solution.py:79
  10.8 58.8 %collective-permute-start.3 = (bf16[4,4,32,2560]{3,2,1,0:T(8,128)(2,1)S(1)}, bf16[4,4,32,2560]{3,2,1,0:T(8,128)(2,1)}, u32[]{:S(2)}, u32[]{:S(2)}) collective-permute-start(bf16[4,4,32,2560]{3,2,1,0:T(8,128)(2,1)S(1)} %broadcast_select_fusion.1), channel_id=1, source_target_pairs={{0,1},{1,0},{2,3},{3,2},{4,5},{5,4},{6,7},{7,6},{8,9},{9,8},{10,11... | collective-permute-start | bytes 7864328 | tf_op jit(solution)/shard_map/ppermute | solution.py:16
  141.4 20.8 %copy-start.2 = (bf16[1,8,4,32,128]{4,3,2,1,0:T(8,128)(2,1)S(1)}, bf16[1,8,4,32,128]{4,3,2,1,0:T(8,128)(2,1)}, u32[]{:S(2)}) copy-start(bf16[1,8,4,32,128]{4,3,2,1,0:T(8,128)(2,1)} %param.5) | copy-start | bytes 786436
  142.3 6.3 %collective-permute-start.5 = (f32[8,1,32,128]{3,2,1,0:T(8,128)S(1)}, f32[8,1,32,128]{3,2,1,0:T(8,128)S(1)}, u32[]{:S(2)}, u32[]{:S(2)}) collective-permute-start(f32[8,1,32,128]{3,2,1,0:T(8,128)S(1)} %get-tuple-element.36), channel_id=1, source_target_pairs={{2,0},{4,2},{6,4},{3,1},{5,3},{7,5},{10,8},{12,10},{14,12},{11,9},... | collective-permute-start | bytes 393224 | tf_op jit(solution)/shard_map/ppermute | solution.py:41
  144.5 5.4 %collective-permute-start.4 = (f32[8,1,32,128]{3,2,1,0:T(8,128)S(1)}, f32[8,1,32,128]{3,2,1,0:T(8,128)S(1)}, u32[]{:S(2)}, u32[]{:S(2)}) collective-permute-start(f32[8,1,32,128]{3,2,1,0:T(8,128)S(1)} %get-tuple-element.35), channel_id=1, source_target_pairs={{0,2},{2,4},{4,6},{1,3},{3,5},{5,7},{8,10},{10,12},{12,14},{9,11},... | collective-permute-start | bytes 393224 | tf_op jit(solution)/shard_map/ppermute | solution.py:41
  150.0 12.2 %collective-permute-start.6 = (f32[8,4,32,128]{3,2,1,0:T(8,128)S(1)}, f32[8,4,32,128]{3,2,1,0:T(8,128)S(1)}, u32[]{:S(2)}, u32[]{:S(2)}) collective-permute-start(f32[8,4,32,128]{3,2,1,0:T(8,128)S(1)} %slice_add_fusion), channel_id=1, source_target_pairs={{0,1},{1,0},{2,3},{3,2},{4,5},{5,4},{6,7},{7,6},{8,9},{9,8},{10,11... | collective-permute-start | bytes 1572872 | tf_op jit(solution)/shard_map/ppermute | solution.py:16
  151.2 19.7 %copy-start.5 = (f32[8]{0:T(128)}, f32[8]{0:T(128)S(1)}, u32[]{:S(2)}) copy-start(f32[8]{0:T(128)S(1)} %compare_convert_fusion) | copy-start | bytes 100
  163.2 5.8 %collective-permute-start.1 = (bf16[8,1,32,128]{3,2,1,0:T(8,128)(2,1)S(1)}, bf16[8,1,32,128]{3,2,1,0:T(8,128)(2,1)S(1)}, u32[]{:S(2)}, u32[]{:S(2)}) collective-permute-start(bf16[8,1,32,128]{3,2,1,0:T(8,128)(2,1)S(1)} %get-tuple-element.43), channel_id=1, source_target_pairs={{2,0},{4,2},{6,4},{3,1},{5,3},{7,5},{10,8},{12,10},{14,12},{11,9},... | collective-permute-start | bytes 196616 | tf_op jit(solution)/shard_map/ppermute | solution.py:41
  165.2 5.0 %collective-permute-start = (bf16[8,1,32,128]{3,2,1,0:T(8,128)(2,1)S(1)}, bf16[8,1,32,128]{3,2,1,0:T(8,128)(2,1)S(1)}, u32[]{:S(2)}, u32[]{:S(2)}) collective-permute-start(bf16[8,1,32,128]{3,2,1,0:T(8,128)(2,1)S(1)} %get-tuple-element.42), channel_id=1, source_target_pairs={{0,2},{2,4},{4,6},{1,3},{3,5},{5,7},{8,10},{10,12},{12,14},{9,11},... | collective-permute-start | bytes 196616 | tf_op jit(solution)/shard_map/ppermute | solution.py:41
  171.1 4.0 %copy-start = (bf16[4,4,32,2560]{3,2,1,0:T(8,128)(2,1)S(1)}, bf16[4,4,32,2560]{3,2,1,0:T(8,128)(2,1)}, u32[]{:S(2)}) copy-start(bf16[4,4,32,2560]{3,2,1,0:T(8,128)(2,1)} %get-tuple-element.32) | copy-start | bytes 7864324
  172.2 2.9 copy-start.3
  196.6 0.7 copy-start.4
  196.6 0.7 copy-start.6
  221.2 2.2 copy-start.1
  221.5 57.9 %collective-permute-start.2 = (bf16[4,4,32,2560]{3,2,1,0:T(8,128)(2,1)S(1)}, bf16[4,4,32,2560]{3,2,1,0:T(8,128)(2,1)S(1)}, u32[]{:S(2)}, u32[]{:S(2)}) collective-permute-start(bf16[4,4,32,2560]{3,2,1,0:T(8,128)(2,1)S(1)} %broadcast_select_fusion.3), channel_id=1, source_target_pairs={{0,1},{1,0},{2,3},{3,2},{4,5},{5,4},{6,7},{7,6},{8,9},{9,8},{10,11... | collective-permute-start | bytes 7864328 | tf_op jit(solution)/shard_map/ppermute | solution.py:16
  225.0 1.2 collective-permute-start.7
  226.2 3.5 collective-permute-start.8
  229.7 2.8 collective-permute-start.9
  232.6 3.4 collective-permute-start.10
Sparse Core Ops, SparseCore 0:
  9.6 95.8 all-gather.1
  196.8 189.0 reduce-scatter.1

commit v2 on v1

--- a/solution.py
+++ b/solution.py
@@ -41,6 +41,33 @@
     return lax.ppermute(high_row, axis, forward), lax.ppermute(low_row, axis, backward)
 
 
+def scatter(value, dim, axis, index, count, stride):
+    total = lax.dynamic_index_in_dim(value, index, dim, keepdims=False)
+    for offset in range(1, count):
+        leaving = lax.dynamic_index_in_dim(value, index ^ offset, dim, keepdims=False)
+        arrived = swap(leaving.astype(jnp.bfloat16), axis, offset * stride)
+        total = total + arrived.astype(jnp.float32)
+    return total
+
+
+def scatter_rows(value, start, width, tile_first):
+    dp, tile = lax.axis_index("dp"), lax.axis_index("tile")
+    dp_count, pair_count = lax.axis_size("dp"), lax.axis_size("tile") // 2
+    value = value.reshape(dp_count, pair_count, 2, -1, value.shape[1])
+    sizes = (dp_count, pair_count, 1, value.shape[3], width)
+
+    def rows_of(parity):
+        return lax.dynamic_slice(value, (0, 0, parity, 0, start), sizes)[:, :, 0]
+
+    arrived = swap(rows_of((tile & 1) ^ 1).astype(jnp.bfloat16), "tile", 1)
+    value = rows_of(tile & 1) + arrived.astype(jnp.float32)
+    if tile_first:
+        value = scatter(value, 1, "tile", tile >> 1, pair_count, 2)
+        return scatter(value, 0, "dp", dp, dp_count, 1)
+    value = scatter(value, 0, "dp", dp, dp_count, 1)
+    return scatter(value, 0, "tile", tile >> 1, pair_count, 2)
+
+
 def silu_grad(values):
     sigma = jax.nn.sigmoid(values)
     return sigma * (1.0 + values * (1.0 - sigma))
@@ -75,16 +102,22 @@
 
     weight_term = lax.dot_general(
         columns, flat_grad, (((0,), (0,)), ((), ())), preferred_element_type=jnp.float32
-    ).astype(jnp.bfloat16)
-    grad_weight = lax.psum_scatter(
-        weight_term, ("dp", "tile"), scatter_dimension=0, tiled=True
-    ).astype(jnp.float32)
+    )
+    half = share // 2
+    grad_weight = jnp.concatenate(
+        [
+            scatter_rows(weight_term, 0, half, True),
+            scatter_rows(weight_term, half, share - half, False),
+        ],
+        axis=1,
+    )
     grad_bias = sum_over(jnp.sum(flat_grad, axis=0, dtype=jnp.float32), ("tile", "dp"))
 
     full_weight = lax.all_gather(weight, ("dp", "tile"), axis=0, tiled=True)
+    bias_vals = bias.astype(jnp.float32) + 0.0 * weight_term[0, 0]
     output = jnp.dot(columns, full_weight, preferred_element_type=jnp.float32)
     tokens = (
-        (output.reshape(frame_count, row_count, col_count, share) + bias.astype(jnp.float32))
+        (output.reshape(frame_count, row_count, col_count, share) + bias_vals)
         * frame_mask
     ).astype(jnp.bfloat16)
     pose_tokens = jnp.concatenate(
@@ -94,9 +127,11 @@
         axis=3,
     )
 
+    after = 0.0 * tokens[0, 0, 0, 0].astype(jnp.float32)
     spread = lax.dot_general(
         flat_grad, full_weight, (((1,), (1,)), ((), ())), preferred_element_type=jnp.float32
-    ).reshape(frame_count, row_count, col_count, 27 * chan_count)
+    )
+    spread = (spread + after).reshape(frame_count, row_count, col_count, 27 * chan_count)
     total = jnp.zeros((frame_count, row_count + 2, col_count, chan_count), jnp.float32)
     for a in range(3):
         for b in range(3):

time: 396 us -> 395 us (level)
  waiting for transfers between devices: 253 us -> 185 us
  other arithmetic: 23.3 us -> 52.1 us
  local copies, waits for them, and re-layouts: 10.9 us -> 31.9 us
  starting transfers between devices: 21.6 us -> 31.6 us
    reduce_scatter x1 -> x0, waiting for transfers between devices: 103 us -> none  [shards(): lax.psum_scatter(weight_term, ('dp', 'tile'), scatter_dimension=0, tiled=...]
    ppermute x7 -> x17, waiting for transfers between devices: 115 us -> 174 us  [swap(): return lax.ppermute(value, axis, [(i, i ^ distance) for i in range(count)])]
    all_gather x1, waiting for transfers between devices: 30.9 us -> 0.01 us  [shards(): full_weight = lax.all_gather(weight, ('dp', 'tile'), axis=0, tiled=True)]
    add x0 -> x7, other arithmetic: none -> 21.5 us  [the longest x2 14.9 us: scatter_rows(): value = rows_of(tile & 1) + arrived.astype(jnp.float32)]
    dynamic_slice x0 -> x1, local copies, waits for them, and re-layouts: none -> 10.6 us  [rows_of(): return lax.dynamic_slice(value, (0, 0, parity, 0, start), sizes)[:, :, 0]]
    ppermute x2, waiting for transfers between devices: 0.63 us -> 9.62 us  [neighbours(): lax.ppermute(low_row, axis, backward)]
    ppermute x7 -> x17, starting transfers between devices: 10.2 us -> 18.6 us  [swap(): return lax.ppermute(value, axis, [(i, i ^ distance) for i in range(count)])]
    concatenate x0 -> x2, other arithmetic: none -> 6.19 us  [the longest x1 4.55 us: shards(): jnp.concatenate(received, axis=0) * frame_mask.astype(jnp.bfloat16)]
  transfers between devices with their start and end apart: 13 -> 22, of which waited for: 12 -> 9; matrix products, arithmetic and copies ran while one was open for 10% -> 39% of each run, Pallas kernels for 0% -> 0%
where the time goes in v2:
time: 395 us; the launch traced here: 391 us
  waiting for transfers between devices  185 us (47%)
  matrix products  74.3 us (19%)
  other arithmetic  52.1 us (13%)
  local copies, waits for them, and re-layouts  31.9 us (8%)
  starting transfers between devices  31.6 us (8%)
  between operations  16.5 us (4%)
    ppermute x17, waiting for transfers between devices, swap(): return lax.ppermute(value, axis, [(i, i ^ distance) for i in range(count)])  174 us
    dot_general x1, matrix products, shards(): lax.dot_general(flat_grad, full_weight, (((1,), (1,)), ((), ())), preferr...  27.5 us
    dot_general x1, matrix products, shards(): output = jnp.dot(columns, full_weight, preferred_element_type=jnp.float32)  23.9 us
    dot_general x1, matrix products, shards(): lax.dot_general(columns, flat_grad, (((0,), (0,)), ((), ())), preferred_e...  22.8 us
    ppermute x17, starting transfers between devices, swap(): return lax.ppermute(value, axis, [(i, i ^ distance) for i in range(count)])  18.6 us
    add x2, other arithmetic, scatter_rows(): value = rows_of(tile & 1) + arrived.astype(jnp.float32)  14.9 us
    dynamic_slice x1, local copies, waits for them, and re-layouts, rows_of(): return lax.dynamic_slice(value, (0, 0, parity, 0, start), sizes)[:, :, 0]  10.6 us
    ppermute x2, waiting for transfers between devices, neighbours(): lax.ppermute(low_row, axis, backward)  9.62 us
  transfers between devices with their start and end apart: 22, of which 9 were waited for; matrix products, arithmetic and copies ran while one was open for 39% of the time, Pallas kernels for 0%

profile of v2, /device:TPU:1, one launch (start us, length us, event | category | flops | bytes accessed | tf_op | source)
XLA Modules:
  0.0 391.1 jit_solution(3623115546137222850)
XLA Ops:
  7.9 2.8 broadcast_select_fusion.3
  10.7 2.2 collective-permute-start.2
  13.8 3.9 %collective-permute-start = (bf16[8,1,32,128]{3,2,1,0:T(8,128)(2,1)S(1)}, bf16[8,1,32,128]{3,2,1,0:T(8,128)(2,1)S(1)}, u32[]{:S(2)}, u32[]{:S(2)}) collective-permute-start(bf16[8,1,32,128]{3,2,1,0:T(8,128)(2,1)S(1)} %get-tuple-element.48), channel_id=1, source_target_pairs={{0,2},{2,4},{4,6},{1,3},{3,5},{5,7},{8,10},{10,12},{12,14},{9,11},... | collective-permute-start | bytes 196616 | tf_op jit(solution)/shard_map/ppermute | solution.py:41
  17.7 1.9 collective-permute-start.1
  20.0 5.1 %collective-permute-done.1 = bf16[8,1,32,128]{3,2,1,0:T(8,128)(2,1)S(1)} collective-permute-done((bf16[8,1,32,128]{3,2,1,0:T(8,128)(2,1)S(1)}, bf16[8,1,32,128]{3,2,1,0:T(8,128)(2,1)S(1)}, u32[]{:S(2)}, u32[]{:S(2)}) %collective-permute-start.1) | collective-permute-done | bytes 65568 | tf_op jit(solution)/shard_map/ppermute | solution.py:41
  27.2 42.4 %collective-permute-done.2 = bf16[4,4,32,2560]{3,2,1,0:T(8,128)(2,1)} collective-permute-done((bf16[4,4,32,2560]{3,2,1,0:T(8,128)(2,1)S(1)}, bf16[4,4,32,2560]{3,2,1,0:T(8,128)(2,1)}, u32[]{:S(2)}, u32[]{:S(2)}) %collective-permute-start.2) | collective-permute-done | bytes 2621472 | tf_op jit(solution)/shard_map/ppermute | solution.py:16
  69.6 2.0 broadcast_select_fusion.6
  71.6 22.8 %fusion.4 = f32[3456,2560,1,1]{1,0,3,2:T(8,128)} fusion(bf16[8,4,32,3456]{3,2,1,0:T(8,128)(2,1)S(1)} %slice_dynamic-update-slice_fusion, bf16[8]{0:T(256)(128)(2,1)S(1)} %fusion.41, bf16[4,4,32,2560]{3,2,1,0:T(8,128)(2,1)S(1)} %get-tuple-element.39, bf16[4,4,32,2560]{3,2,1,0:T(8,128)(2,1)S(1)} %get-tuple-element.38), kind=kOutput, calls=%fused_computation.12 | convolution fusion | flops 18124636160 | bytes 47710224 | tf_op jit(solution)/shard_map/dot_general | solution.py:103
  94.5 10.6 %constant_dynamic-slice_fusion = (bf16[4,2,1,216,1280]{4,3,2,1,0:T(8,128)(2,1)}, bf16[4,2,216,1280]{3,2,1,0:T(8,128)(2,1)}) fusion(f32[4,2,2,216,2560]{4,3,2,1,0:T(8,128)} %bitcast.86, s32[]{:T(128)S(6)} %select_n.85), kind=kLoop, calls=%fused_computation.107 | loop fusion | bytes 17694724 | tf_op jit(solution)/shard_map/dynamic_slice | solution.py:60
  105.0 4.7 %copy.20 = bf16[4,2,1,216,1280]{4,3,0,1,2:T(8,128)(2,1)} copy(bf16[4,2,1,216,1280]{4,3,2,1,0:T(8,128)(2,1)} %get-tuple-element.4) | data formatting | bytes 8847360
  113.3 4.8 %collective-permute-done.17 = f32[2560]{0:T(1024)S(1)} collective-permute-done((f32[2560]{0:T(1024)S(1)}, f32[2560]{0:T(1024)S(1)}, u32[]{:S(2)}, u32[]{:S(2)}) %collective-permute-start.17) | collective-permute-done | bytes 10272 | tf_op jit(solution)/shard_map/ppermute | solution.py:16
  119.5 4.5 %pad_maximum_fusion = bf16[8,4,32,2560]{3,2,1,0:T(8,128)(2,1)} fusion(bf16[4,4,32,2560]{3,2,1,0:T(8,128)(2,1)} %copy-done, bf16[4,4,32,2560]{3,2,1,0:T(8,128)(2,1)S(1)} %get-tuple-element.38), kind=kLoop, calls=%fused_computation.9 | loop fusion | flops 2621440 | bytes 10485760 | tf_op jit(solution)/shard_map/concatenate | solution.py:89
  125.4 5.7 %bitcast_add_fusion.1 = f32[4,2,216,1280]{3,2,0,1:T(8,128)S(1)} fusion(bf16[4,2,216,1280]{3,2,0,1:T(8,128)(2,1)} %collective-permute-done.7, f32[4,2,2,216,2560]{4,3,2,1,0:T(8,128)} %bitcast.87, s32[]{:T(128)S(6)} %select_n.84), kind=kLoop, calls=%fused_computation.8 | loop fusion | flops 4423680 | bytes 22118404 | tf_op jit(solution)/shard_map/add | solution.py:63
  132.9 9.2 %bitcast_add_fusion = f32[4,2,216,1280]{3,2,1,0:T(8,128)} fusion(bf16[4,2,216,1280]{3,2,1,0:T(8,128)(2,1)} %collective-permute-done.12, f32[4,2,2,216,2560]{4,3,2,1,0:T(8,128)} %bitcast.88, s32[]{:T(128)S(6)} %select_n.84), kind=kLoop, calls=%fused_computation.7 | loop fusion | flops 4423680 | bytes 22118404 | tf_op jit(solution)/shard_map/add | solution.py:63
  142.0 3.3 fusion.15
  145.4 2.4 collective-permute-start.14
  149.0 5.2 %bitcast_multiply_fusion = bf16[1024,2560]{1,0:T(8,128)(2,1)} fusion(bf16[8,4,32,2560]{3,2,1,0:T(8,128)(2,1)} %pad_maximum_fusion, bf16[1024]{0:T(1024)(128)(2,1)S(1)} %mul.77), kind=kLoop, calls=%fused_computation.11 | loop fusion | flops 2621440 | bytes 10487808 | tf_op jit(solution)/shard_map/mul | solution.py:89
  157.5 84.8 %collective-permute-done.20 = f32[2560]{0:T(1024)S(1)} collective-permute-done((f32[2560]{0:T(1024)S(1)}, f32[2560]{0:T(1024)S(1)}, u32[]{:S(2)}, u32[]{:S(2)}) %collective-permute-start.20) | collective-permute-done | bytes 10272 | tf_op jit(solution)/shard_map/ppermute | solution.py:16
  242.9 2.2 fusion.11
  247.3 4.1 %bitcast_add_fusion.2 = f32[4,216,1280]{2,1,0:T(8,128)} fusion(bf16[4,216,1280]{2,1,0:T(8,128)(2,1)} %collective-permute-done.8, f32[4,2,216,1280]{3,2,0,1:T(8,128)S(1)} %bitcast_add_fusion.1, s32[]{:T(128)S(6)} %select_n.86), kind=kLoop, calls=%fused_computation.16 | loop fusion | flops 2211840 | bytes 11059204 | tf_op jit(solution)/shard_map/add | solution.py:49
  251.4 23.9 %multiply_convert_fusion = bf16[8,4,32,2560]{3,2,1,0:T(8,128)(2,1)S(1)} fusion(bf16[8,4,32,3456]{3,2,1,0:T(8,128)(2,1)} %copy-done.6, bf16[3456,2560]{1,0:T(8,128)(2,1)} %all-gather.2.cloned.1.call-done, f32[8]{0:T(128)S(1)} %copy-done.9, f32[2560]{0:T(1024)S(1)} %convert_add_fusion), kind=kOutput, calls=%fused_computation.3 | convolution fusion | flops 18127257600 | bytes 30025760 | tf_op jit(solution)/shard_map/dot_general | solution.py:118
  277.6 1.8 broadcast_select_fusion.1
  280.1 27.5 %convolution_add_fusion = f32[1024,3456]{1,0:T(8,128)} fusion(bf16[1024,2560]{1,0:T(8,128)(2,1)} %bitcast_multiply_fusion, bf16[3456,2560]{1,0:T(8,128)(2,1)} %all-gather.2.cloned.1.call-done, f32[]{:T(128)} %bitcast.11), kind=kOutput, calls=%fused_computation.4 | convolution fusion | flops 18122932224 | bytes 37093380 | tf_op jit(solution)/shard_map/dot_general | solution.py:131
  307.6 5.2 %fusion.42 = (f32[8,4,31,128]{3,2,1,0:T(8,128)S(1)}, f32[8,4,31,128]{3,2,1,0:T(8,128)S(1)}, f32[8,4,31,128]{3,2,1,0:T(8,128)S(1)}, f32[8,4,31,128]{3,2,1,0:T(8,1...) fusion(f32[8,4,32,3456]{3,2,1,0:T(8,128)} %bitcast.90), kind=kLoop, calls=%fused_computation.111 | loop fusion | bytes 18284544 | tf_op jit(solution)/shard_map/slice | solution.py:144
  314.1 3.4 fusion.43
  319.2 5.2 %collective-permute-start.4 = (f32[8,1,32,128]{3,2,1,0:T(8,128)S(1)}, f32[8,1,32,128]{3,2,1,0:T(8,128)S(1)}, u32[]{:S(2)}, u32[]{:S(2)}) collective-permute-start(f32[8,1,32,128]{3,2,1,0:T(8,128)S(1)} %get-tuple-element.43), channel_id=1, source_target_pairs={{0,2},{2,4},{4,6},{1,3},{3,5},{5,7},{8,10},{10,12},{12,14},{9,11},... | collective-permute-start | bytes 393224 | tf_op jit(solution)/shard_map/ppermute | solution.py:41
  328.4 1.9 collective-permute-start.5
  330.5 4.5 %collective-permute-done.5 = f32[8,1,32,128]{3,2,1,0:T(8,128)S(1)} collective-permute-done((f32[8,1,32,128]{3,2,1,0:T(8,128)S(1)}, f32[8,1,32,128]{3,2,1,0:T(8,128)S(1)}, u32[]{:S(2)}, u32[]{:S(2)}) %collective-permute-start.5) | collective-permute-done | bytes 131104 | tf_op jit(solution)/shard_map/ppermute | solution.py:41
  335.4 28.3 %collective-permute-done.10 = bf16[216,1280]{1,0:T(8,128)(2,1)S(1)} collective-permute-done((bf16[216,1280]{1,0:T(8,128)(2,1)S(1)}, bf16[216,1280]{1,0:T(8,128)(2,1)S(1)}, u32[]{:S(2)}, u32[]{:S(2)}) %collective-permute-start.10) | collective-permute-done | bytes 552992 | tf_op jit(solution)/shard_map/ppermute | solution.py:16
  363.7 1.9 collective-permute-done.9
  367.5 12.0 %collective-permute-done.6 = f32[8,4,32,128]{3,2,1,0:T(8,128)S(1)} collective-permute-done((f32[8,4,32,128]{3,2,1,0:T(8,128)S(1)}, f32[8,4,32,128]{3,2,1,0:T(8,128)S(1)}, u32[]{:S(2)}, u32[]{:S(2)}) %collective-permute-start.6) | collective-permute-done | bytes 524320 | tf_op jit(solution)/shard_map/ppermute | solution.py:16
  381.2 3.0 maximum_bitcast_fusion
  (108 shorter events, 31.4 us)
Async XLA Ops:
  7.2 6.4 %copy-start.4 = (bf16[1,8,4,32,128]{4,3,2,1,0:T(8,128)(2,1)S(1)}, bf16[1,8,4,32,128]{4,3,2,1,0:T(8,128)(2,1)}, u32[]{:S(2)}) copy-start(bf16[1,8,4,32,128]{4,3,2,1,0:T(8,128)(2,1)} %param.5) | copy-start | bytes 786436
  7.2 244.2 %all-gather.2.cloned.1.call-start = ((), (), s32[]{:S(2)}) async-start(), calls=%async_computation | async-start | bytes 18800640 | tf_op jit(solution)/shard_map/all_gather | solution.py:116
  10.7 58.8 %collective-permute-start.2 = (bf16[4,4,32,2560]{3,2,1,0:T(8,128)(2,1)S(1)}, bf16[4,4,32,2560]{3,2,1,0:T(8,128)(2,1)}, u32[]{:S(2)}, u32[]{:S(2)}) collective-permute-start(bf16[4,4,32,2560]{3,2,1,0:T(8,128)(2,1)S(1)} %broadcast_select_fusion.3), channel_id=1, source_target_pairs={{0,1},{1,0},{2,3},{3,2},{4,5},{5,4},{6,7},{7,6},{8,9},{9,8},{10,11... | collective-permute-start | bytes 7864328 | tf_op jit(solution)/shard_map/ppermute | solution.py:16
  13.8 6.2 %collective-permute-start = (bf16[8,1,32,128]{3,2,1,0:T(8,128)(2,1)S(1)}, bf16[8,1,32,128]{3,2,1,0:T(8,128)(2,1)S(1)}, u32[]{:S(2)}, u32[]{:S(2)}) collective-permute-start(bf16[8,1,32,128]{3,2,1,0:T(8,128)(2,1)S(1)} %get-tuple-element.48), channel_id=1, source_target_pairs={{0,2},{2,4},{4,6},{1,3},{3,5},{5,7},{8,10},{10,12},{12,14},{9,11},... | collective-permute-start | bytes 196616 | tf_op jit(solution)/shard_map/ppermute | solution.py:41
  17.7 7.4 %collective-permute-start.1 = (bf16[8,1,32,128]{3,2,1,0:T(8,128)(2,1)S(1)}, bf16[8,1,32,128]{3,2,1,0:T(8,128)(2,1)S(1)}, u32[]{:S(2)}, u32[]{:S(2)}) collective-permute-start(bf16[8,1,32,128]{3,2,1,0:T(8,128)(2,1)S(1)} %get-tuple-element.49), channel_id=1, source_target_pairs={{2,0},{4,2},{6,4},{3,1},{5,3},{7,5},{10,8},{12,10},{14,12},{11,9},... | collective-permute-start | bytes 196616 | tf_op jit(solution)/shard_map/ppermute | solution.py:41
  25.8 43.7 %slice-start = ((s8[5242880]{0:T(1024)(128)(4,1)}), s8[4194304]{0:T(1024)(128)(4,1)S(1)}, s32[]{:S(2)}) async-start(s8[5242880]{0:T(1024)(128)(4,1)} %bitcast.81), calls=%async_computation.1 | async-start | bytes 8388608
  26.4 43.2 %slice-start.1 = ((s8[5242880]{0:T(1024)(128)(4,1)}), s8[1048576]{0:T(1024)(128)(4,1)S(1)}, s32[]{:S(2)}) async-start(s8[5242880]{0:T(1024)(128)(4,1)} %bitcast.81), calls=%async_computation.2 | async-start | bytes 2097152
  27.2 44.4 %copy-start.6 = (bf16[8,4,32,3456]{3,2,1,0:T(8,128)(2,1)}, bf16[8,4,32,3456]{3,2,1,0:T(8,128)(2,1)S(1)}, u32[]{:S(2)}) copy-start(bf16[8,4,32,3456]{3,2,1,0:T(8,128)(2,1)S(1)} %slice_dynamic-update-slice_fusion) | copy-start | bytes 21233668
  71.6 22.9 %copy-start = (bf16[4,4,32,2560]{3,2,1,0:T(8,128)(2,1)}, bf16[4,4,32,2560]{3,2,1,0:T(8,128)(2,1)S(1)}, u32[]{:S(2)}) copy-start(bf16[4,4,32,2560]{3,2,1,0:T(8,128)(2,1)S(1)} %get-tuple-element.39) | copy-start | bytes 7864324
  109.7 15.7 %collective-permute-start.7 = (bf16[4,2,216,1280]{3,2,0,1:T(8,128)(2,1)}, bf16[4,2,216,1280]{3,2,0,1:T(8,128)(2,1)}, u32[]{:S(2)}, u32[]{:S(2)}) collective-permute-start(bf16[4,2,216,1280]{3,2,0,1:T(8,128)(2,1)} %bitcast.77), channel_id=1, source_target_pairs={{0,2},{2,0},{4,6},{6,4},{1,3},{3,1},{5,7},{7,5},{8,10},{10,8},{12,... | collective-permute-start | bytes 13271048 | tf_op jit(solution)/shard_map/ppermute | solution.py:16
  110.9 21.9 %collective-permute-start.12 = (bf16[4,2,216,1280]{3,2,1,0:T(8,128)(2,1)}, bf16[4,2,216,1280]{3,2,1,0:T(8,128)(2,1)}, u32[]{:S(2)}, u32[]{:S(2)}) collective-permute-start(bf16[4,2,216,1280]{3,2,1,0:T(8,128)(2,1)} %get-tuple-element.5), channel_id=1, source_target_pairs={{0,2},{2,0},{4,6},{6,4},{1,3},{3,1},{5,7},{7,5},{8,10},{10,8},{12,... | collective-permute-start | bytes 13271048 | tf_op jit(solution)/shard_map/ppermute | solution.py:16
  112.5 5.6 %collective-permute-start.17 = (f32[2560]{0:T(1024)S(1)}, f32[2560]{0:T(1024)S(1)}, u32[]{:S(2)}, u32[]{:S(2)}) collective-permute-start(f32[2560]{0:T(1024)S(1)} %convert_reduce_fusion), channel_id=1, source_target_pairs={{0,2},{2,0},{4,6},{6,4},{1,3},{3,1},{5,7},{7,5},{8,10},{10,8},{12,... | collective-permute-start | bytes 30728 | tf_op jit(solution)/shard_map/ppermute | solution.py:16
  118.1 6.0 %collective-permute-start.18 = (f32[2560]{0:T(1024)S(1)}, f32[2560]{0:T(1024)S(1)}, u32[]{:S(2)}, u32[]{:S(2)}) collective-permute-start(f32[2560]{0:T(1024)S(1)} %add.300), channel_id=1, source_target_pairs={{0,4},{2,6},{4,0},{6,2},{1,5},{3,7},{5,1},{7,3},{8,12},{10,14},{12... | collective-permute-start | bytes 30728 | tf_op jit(solution)/shard_map/ppermute | solution.py:16
  124.1 31.9 %collective-permute-start.19 = (f32[2560]{0:T(1024)S(1)}, f32[2560]{0:T(1024)S(1)}, u32[]{:S(2)}, u32[]{:S(2)}) collective-permute-start(f32[2560]{0:T(1024)S(1)} %add.301), channel_id=1, source_target_pairs={{0,8},{8,0},{16,24},{24,16},{1,9},{9,1},{17,25},{25,17},{2,10},{10... | collective-permute-start | bytes 30728 | tf_op jit(solution)/shard_map/ppermute | solution.py:16
  132.7 114.6 %collective-permute-start.8 = (bf16[4,216,1280]{2,1,0:T(8,128)(2,1)}, bf16[4,216,1280]{2,1,0:T(8,128)(2,1)}, u32[]{:S(2)}, u32[]{:S(2)}) collective-permute-start(bf16[4,216,1280]{2,1,0:T(8,128)(2,1)} %fusion.9), channel_id=1, source_target_pairs={{0,4},{2,6},{4,0},{6,2},{1,5},{3,7},{5,1},{7,3},{8,12},{10,14},{12... | collective-permute-start | bytes 6635528 | tf_op jit(solution)/shard_map/ppermute | solution.py:16
  145.3 97.6 %collective-permute-start.13 = (bf16[2,216,1280]{2,1,0:T(8,128)(2,1)S(1)}, bf16[2,216,1280]{2,1,0:T(8,128)(2,1)S(1)}, u32[]{:S(2)}, u32[]{:S(2)}) collective-permute-start(bf16[2,216,1280]{2,1,0:T(8,128)(2,1)S(1)} %get-tuple-element.33), channel_id=1, source_target_pairs={{0,8},{8,0},{16,24},{24,16},{1,9},{9,1},{17,25},{25,17},{2,10},{10... | collective-permute-start | bytes 3317768 | tf_op jit(solution)/shard_map/ppermute | solution.py:16
  145.4 97.5 %collective-permute-start.14 = (bf16[2,216,1280]{2,1,0:T(8,128)(2,1)S(1)}, bf16[2,216,1280]{2,1,0:T(8,128)(2,1)S(1)}, u32[]{:S(2)}, u32[]{:S(2)}) collective-permute-start(bf16[2,216,1280]{2,1,0:T(8,128)(2,1)S(1)} %get-tuple-element.35), channel_id=1, source_target_pairs={{0,16},{8,24},{16,0},{24,8},{1,17},{9,25},{17,1},{25,9},{2,18},{10... | collective-permute-start | bytes 3317768 | tf_op jit(solution)/shard_map/ppermute | solution.py:16
  147.9 9.7 %copy-start.7 = (bf16[2560]{0:T(1024)(128)(2,1)S(1)}, bf16[2560]{0:T(1024)(128)(2,1)}, u32[]{:S(2)}) copy-start(bf16[2560]{0:T(1024)(128)(2,1)} %param.8) | copy-start | bytes 15364
  147.9 95.0 %collective-permute-start.15 = (bf16[2,216,1280]{2,1,0:T(8,128)(2,1)S(1)}, bf16[2,216,1280]{2,1,0:T(8,128)(2,1)S(1)}, u32[]{:S(2)}, u32[]{:S(2)}) collective-permute-start(bf16[2,216,1280]{2,1,0:T(8,128)(2,1)S(1)} %get-tuple-element.34), channel_id=1, source_target_pairs={{0,24},{8,16},{16,8},{24,0},{1,25},{9,17},{17,9},{25,1},{2,26},{10... | collective-permute-start | bytes 3317768 | tf_op jit(solution)/shard_map/ppermute | solution.py:16
  156.0 86.3 %collective-permute-start.20 = (f32[2560]{0:T(1024)S(1)}, f32[2560]{0:T(1024)S(1)}, u32[]{:S(2)}, u32[]{:S(2)}) collective-permute-start(f32[2560]{0:T(1024)S(1)} %add.302), channel_id=1, source_target_pairs={{0,16},{8,24},{16,0},{24,8},{1,17},{9,25},{17,1},{25,9},{2,18},{10... | collective-permute-start | bytes 30728 | tf_op jit(solution)/shard_map/ppermute | solution.py:16
  246.0 82.2 %collective-permute-start.16 = (bf16[216,1280]{1,0:T(8,128)(2,1)}, bf16[216,1280]{1,0:T(8,128)(2,1)S(1)}, u32[]{:S(2)}, u32[]{:S(2)}) collective-permute-start(bf16[216,1280]{1,0:T(8,128)(2,1)} %fusion.26), channel_id=1, source_target_pairs={{0,4},{2,6},{4,0},{6,2},{1,5},{3,7},{5,1},{7,3},{8,12},{10,14},{12... | collective-permute-start | bytes 1658888 | tf_op jit(solution)/shard_map/ppermute | solution.py:16
  312.8 67.7 %collective-permute-start.3 = (bf16[4,4,32,2560]{3,2,1,0:T(8,128)(2,1)S(1)}, bf16[4,4,32,2560]{3,2,1,0:T(8,128)(2,1)S(1)}, u32[]{:S(2)}, u32[]{:S(2)}) collective-permute-start(bf16[4,4,32,2560]{3,2,1,0:T(8,128)(2,1)S(1)} %copy-done.3), channel_id=1, source_target_pairs={{0,1},{1,0},{2,3},{3,2},{4,5},{5,4},{6,7},{7,6},{8,9},{9,8},{10,11... | collective-permute-start | bytes 7864328 | tf_op jit(solution)/shard_map/ppermute | solution.py:16
  317.9 6.6 %slice-start.4 = ((s8[4423680]{0:T(1024)(128)(4,1)}), s8[4194304]{0:T(1024)(128)(4,1)S(1)}, s32[]{:S(2)}) async-start(s8[4423680]{0:T(1024)(128)(4,1)} %bitcast.92), calls=%async_computation.5 | async-start | bytes 8388608
  319.2 9.2 %collective-permute-start.4 = (f32[8,1,32,128]{3,2,1,0:T(8,128)S(1)}, f32[8,1,32,128]{3,2,1,0:T(8,128)S(1)}, u32[]{:S(2)}, u32[]{:S(2)}) collective-permute-start(f32[8,1,32,128]{3,2,1,0:T(8,128)S(1)} %get-tuple-element.43), channel_id=1, source_target_pairs={{0,2},{2,4},{4,6},{1,3},{3,5},{5,7},{8,10},{10,12},{12,14},{9,11},... | collective-permute-start | bytes 393224 | tf_op jit(solution)/shard_map/ppermute | solution.py:41
  324.7 39.0 %collective-permute-start.10 = (bf16[216,1280]{1,0:T(8,128)(2,1)S(1)}, bf16[216,1280]{1,0:T(8,128)(2,1)S(1)}, u32[]{:S(2)}, u32[]{:S(2)}) collective-permute-start(bf16[216,1280]{1,0:T(8,128)(2,1)S(1)} %get-tuple-element.42), channel_id=1, source_target_pairs={{0,16},{8,24},{16,0},{24,8},{1,17},{9,25},{17,1},{25,9},{2,18},{10... | collective-permute-start | bytes 1658888 | tf_op jit(solution)/shard_map/ppermute | solution.py:16
  326.5 37.2 %collective-permute-start.11 = (bf16[216,1280]{1,0:T(8,128)(2,1)S(1)}, bf16[216,1280]{1,0:T(8,128)(2,1)S(1)}, u32[]{:S(2)}, u32[]{:S(2)}) collective-permute-start(bf16[216,1280]{1,0:T(8,128)(2,1)S(1)} %get-tuple-element.41), channel_id=1, source_target_pairs={{0,24},{8,16},{16,8},{24,0},{1,25},{9,17},{17,9},{25,1},{2,26},{10... | collective-permute-start | bytes 1658888 | tf_op jit(solution)/shard_map/ppermute | solution.py:16
  328.2 37.4 %collective-permute-start.9 = (bf16[216,1280]{1,0:T(8,128)(2,1)S(1)}, bf16[216,1280]{1,0:T(8,128)(2,1)S(1)}, u32[]{:S(2)}, u32[]{:S(2)}) collective-permute-start(bf16[216,1280]{1,0:T(8,128)(2,1)S(1)} %get-tuple-element.40), channel_id=1, source_target_pairs={{0,8},{8,0},{16,24},{24,16},{1,9},{9,1},{17,25},{25,17},{2,10},{10... | collective-permute-start | bytes 1658888 | tf_op jit(solution)/shard_map/ppermute | solution.py:16
  328.4 6.6 %collective-permute-start.5 = (f32[8,1,32,128]{3,2,1,0:T(8,128)S(1)}, f32[8,1,32,128]{3,2,1,0:T(8,128)S(1)}, u32[]{:S(2)}, u32[]{:S(2)}) collective-permute-start(f32[8,1,32,128]{3,2,1,0:T(8,128)S(1)} %get-tuple-element.44), channel_id=1, source_target_pairs={{2,0},{4,2},{6,4},{3,1},{5,3},{7,5},{10,8},{12,10},{14,12},{11,9},... | collective-permute-start | bytes 393224 | tf_op jit(solution)/shard_map/ppermute | solution.py:41
  330.3 50.2 %slice-start.2 = ((s8[5242880]{0:T(1024)(128)(4,1)}), s8[4194304]{0:T(1024)(128)(4,1)S(1)}, s32[]{:S(2)}) async-start(s8[5242880]{0:T(1024)(128)(4,1)} %bitcast.84), calls=%async_computation.3 | async-start | bytes 8388608
  335.1 44.4 %copy-start.5 = (bf16[1,8,4,32,128]{4,3,2,1,0:T(8,128)(2,1)S(1)}, bf16[1,8,4,32,128]{4,3,2,1,0:T(8,128)(2,1)}, u32[]{:S(2)}) copy-start(bf16[1,8,4,32,128]{4,3,2,1,0:T(8,128)(2,1)} %param.5) | copy-start | bytes 786436
  335.1 45.4 %slice-start.3 = ((s8[5242880]{0:T(1024)(128)(4,1)}), s8[1048576]{0:T(1024)(128)(4,1)S(1)}, s32[]{:S(2)}) async-start(s8[5242880]{0:T(1024)(128)(4,1)} %bitcast.84), calls=%async_computation.4 | async-start | bytes 2097152
  335.1 44.4 %collective-permute-start.6 = (f32[8,4,32,128]{3,2,1,0:T(8,128)S(1)}, f32[8,4,32,128]{3,2,1,0:T(8,128)S(1)}, u32[]{:S(2)}, u32[]{:S(2)}) collective-permute-start(f32[8,4,32,128]{3,2,1,0:T(8,128)S(1)} %slice_add_fusion), channel_id=1, source_target_pairs={{0,1},{1,0},{2,3},{3,2},{4,5},{5,4},{6,7},{7,6},{8,9},{9,8},{10,11... | collective-permute-start | bytes 1572872 | tf_op jit(solution)/shard_map/ppermute | solution.py:16
  (6 other events, 29.2 us)
Sparse Core Ops, SparseCore 0:
  9.6 96.3 all-gather.1

commit v3 on v2

--- a/solution.py
+++ b/solution.py
@@ -41,17 +41,23 @@
     return lax.ppermute(high_row, axis, forward), lax.ppermute(low_row, axis, backward)
 
 
-def scatter(value, dim, axis, index, count, stride):
-    total = lax.dynamic_index_in_dim(value, index, dim, keepdims=False)
+def scatter_start(value, dim, axis, index, count, stride):
+    terms = [lax.dynamic_index_in_dim(value, index, dim, keepdims=False)]
     for offset in range(1, count):
         leaving = lax.dynamic_index_in_dim(value, index ^ offset, dim, keepdims=False)
-        arrived = swap(leaving.astype(jnp.bfloat16), axis, offset * stride)
-        total = total + arrived.astype(jnp.float32)
+        terms.append(swap(leaving.astype(jnp.bfloat16), axis, offset * stride))
+    return terms
+
+
+def scatter_end(terms, after):
+    total = terms[0] + after
+    for term in terms[1:]:
+        total = total + term.astype(jnp.float32)
     return total
 
 
-def scatter_rows(value, start, width, tile_first):
-    dp, tile = lax.axis_index("dp"), lax.axis_index("tile")
+def pair_rows(value, start, width):
+    tile = lax.axis_index("tile")
     dp_count, pair_count = lax.axis_size("dp"), lax.axis_size("tile") // 2
     value = value.reshape(dp_count, pair_count, 2, -1, value.shape[1])
     sizes = (dp_count, pair_count, 1, value.shape[3], width)
@@ -60,12 +66,16 @@
         return lax.dynamic_slice(value, (0, 0, parity, 0, start), sizes)[:, :, 0]
 
     arrived = swap(rows_of((tile & 1) ^ 1).astype(jnp.bfloat16), "tile", 1)
-    value = rows_of(tile & 1) + arrived.astype(jnp.float32)
-    if tile_first:
-        value = scatter(value, 1, "tile", tile >> 1, pair_count, 2)
-        return scatter(value, 0, "dp", dp, dp_count, 1)
-    value = scatter(value, 0, "dp", dp, dp_count, 1)
-    return scatter(value, 0, "tile", tile >> 1, pair_count, 2)
+    return rows_of(tile & 1) + arrived.astype(jnp.float32)
+
+
+def scatter_tile(value):
+    tile = lax.axis_index("tile")
+    return scatter_start(value, value.ndim - 3, "tile", tile >> 1, lax.axis_size("tile") // 2, 2)
+
+
+def scatter_dp(value):
+    return scatter_start(value, 0, "dp", lax.axis_index("dp"), lax.axis_size("dp"), 1)
 
 
 def silu_grad(values):
@@ -103,15 +113,14 @@
     weight_term = lax.dot_general(
         columns, flat_grad, (((0,), (0,)), ((), ())), preferred_element_type=jnp.float32
     )
-    half = share // 2
-    grad_weight = jnp.concatenate(
-        [
-            scatter_rows(weight_term, 0, half, True),
-            scatter_rows(weight_term, half, share - half, False),
-        ],
-        axis=1,
-    )
-    grad_bias = sum_over(jnp.sum(flat_grad, axis=0, dtype=jnp.float32), ("tile", "dp"))
+    units = share // 128
+    last = max(1, units * 3 // 10)
+    first = (units - last) // 2
+    widths = [128 * first, 128 * (units - last - first), 128 * last]
+    starts = [0, widths[0], widths[0] + widths[1]]
+    partials = [pair_rows(weight_term, c, w) for c, w in zip(starts, widths)]
+    moving = [scatter_tile(partials[0]), scatter_dp(partials[2]), scatter_tile(partials[1])]
+    grad_bias = lax.psum(jnp.sum(flat_grad, axis=0, dtype=jnp.float32), ("dp", "tile"))
 
     full_weight = lax.all_gather(weight, ("dp", "tile"), axis=0, tiled=True)
     bias_vals = bias.astype(jnp.float32) + 0.0 * weight_term[0, 0]
@@ -131,7 +140,15 @@
     spread = lax.dot_general(
         flat_grad, full_weight, (((1,), (1,)), ((), ())), preferred_element_type=jnp.float32
     )
+    moving = [
+        scatter_dp(scatter_end(moving[0], after)),
+        scatter_tile(scatter_end(moving[1], after)),
+        scatter_dp(scatter_end(moving[2], after)),
+    ]
     spread = (spread + after).reshape(frame_count, row_count, col_count, 27 * chan_count)
+    late = 0.0 * spread[0, 0, 0, 0]
+    ended = [scatter_end(terms, late) for terms in moving]
+    grad_weight = jnp.concatenate([ended[0], ended[2], ended[1]], axis=1)
     total = jnp.zeros((frame_count, row_count + 2, col_count, chan_count), jnp.float32)
     for a in range(3):
         for b in range(3):

time: 395 us -> 377 us (0.954)
  waiting for transfers between devices: 185 us -> 98.7 us
  blocking collectives: 0 us -> 58.2 us
  local copies, waits for them, and re-layouts: 31.9 us -> 48.2 us
  other arithmetic: 52.1 us -> 44.2 us
    ppermute x17 -> x18, waiting for transfers between devices: 174 us -> 92.8 us  [swap(): return lax.ppermute(value, axis, [(i, i ^ distance) for i in range(count)])]
    psum x0 -> x1, blocking collectives: none -> 58.2 us  [shards(): lax.psum(jnp.sum(flat_grad, axis=0, dtype=jnp.float32), ('dp', 'tile'))]
    add x10 -> x9, other arithmetic: 22.2 us -> 16.2 us  [the longest x3 9.41 us: pair_rows(): return rows_of(tile & 1) + arrived.astype(jnp.float32)]
    unnamed x41 -> x70, local copies, waits for them, and re-layouts: 7.69 us -> 12.9 us
    dynamic_slice x1 -> x2, local copies, waits for them, and re-layouts: 10.6 us -> 15.1 us  [rows_of(): return lax.dynamic_slice(value, (0, 0, parity, 0, start), sizes)[:, :, 0]]
    ppermute x2, waiting for transfers between devices: 9.62 us -> 5.18 us  [neighbours(): lax.ppermute(low_row, axis, backward)]
    convert_element_type x4 -> x7, local copies, waits for them, and re-layouts: 6.01 us -> 8.74 us  [the longest x6 4.4 us: scatter_start(): terms.append(swap(leaving.astype(jnp.bfloat16), axis, offset * stride))]
    ppermute x17 -> x18, starting transfers between devices: 18.6 us -> 17.5 us  [swap(): return lax.ppermute(value, axis, [(i, i ^ distance) for i in range(count)])]
  transfers between devices with their start and end apart: 22 -> 23, of which waited for: 9 -> 5; matrix products, arithmetic and copies ran while one was open for 39% -> 42% of each run, Pallas kernels for 0% -> 0%
where the time goes in v3:
time: 377 us
  waiting for transfers between devices  98.7 us (26%)
  matrix products  77.4 us (21%)
  blocking collectives  58.2 us (15%)
  local copies, waits for them, and re-layouts  48.2 us (13%)
  other arithmetic  44.2 us (12%)
  starting transfers between devices  32.7 us (9%)
  between operations  17.3 us (5%)
    ppermute x18, waiting for transfers between devices, swap(): return lax.ppermute(value, axis, [(i, i ^ distance) for i in range(count)])  92.8 us
    psum x1, blocking collectives, shards(): lax.psum(jnp.sum(flat_grad, axis=0, dtype=jnp.float32), ('dp', 'tile'))  58.2 us
    dot_general x1, matrix products, shards(): lax.dot_general(flat_grad, full_weight, (((1,), (1,)), ((), ())), preferr...  27.2 us
    dot_general x1, matrix products, shards(): lax.dot_general(columns, flat_grad, (((0,), (0,)), ((), ())), preferred_e...  26.3 us
    dot_general x1, matrix products, shards(): output = jnp.dot(columns, full_weight, preferred_element_type=jnp.float32)  23.9 us
    ppermute x18, starting transfers between devices, swap(): return lax.ppermute(value, axis, [(i, i ^ distance) for i in range(count)])  17.5 us
    dynamic_slice x2, local copies, waits for them, and re-layouts, rows_of(): return lax.dynamic_slice(value, (0, 0, parity, 0, start), sizes)[:, :, 0]  15.1 us
    unnamed x70, local copies, waits for them, and re-layouts  12.9 us
  transfers between devices with their start and end apart: 23, of which 5 were waited for; matrix products, arithmetic and copies ran while one was open for 42% of the time, Pallas kernels for 0%

profile of v3, /device:TPU:1, one launch (start us, length us, event | category | flops | bytes accessed | tf_op | source)
XLA Modules:
  0.0 376.7 jit_solution(2921561220971921254)
XLA Ops:
  9.7 4.5 %collective-permute-start = (bf16[8,1,32,128]{3,2,1,0:T(8,128)(2,1)S(1)}, bf16[8,1,32,128]{3,2,1,0:T(8,128)(2,1)S(1)}, u32[]{:S(2)}, u32[]{:S(2)}) collective-permute-start(bf16[8,1,32,128]{3,2,1,0:T(8,128)(2,1)S(1)} %get-tuple-element.53), channel_id=1, source_target_pairs={{0,2},{2,4},{4,6},{1,3},{3,5},{5,7},{8,10},{10,12},{12,14},{9,11},... | collective-permute-start | bytes 196616 | tf_op jit(solution)/shard_map/ppermute | solution.py:41
  14.2 1.9 collective-permute-start.1
  16.2 2.8 broadcast_select_fusion.3
  23.8 2.8 copy-done.12
  26.6 49.5 %collective-permute-done.2 = bf16[4,4,32,2560]{3,2,1,0:T(8,128)(2,1)} collective-permute-done((bf16[4,4,32,2560]{3,2,1,0:T(8,128)(2,1)S(1)}, bf16[4,4,32,2560]{3,2,1,0:T(8,128)(2,1)}, u32[]{:S(2)}, u32[]{:S(2)}) %collective-permute-start.2) | collective-permute-done | bytes 2621472 | tf_op jit(solution)/shard_map/ppermute | solution.py:16
  76.1 2.3 broadcast_select_fusion.6
  78.4 26.3 %fusion.4 = f32[3456,2560,1,1]{1,0,3,2:T(8,128)} fusion(bf16[8,4,32,3456]{3,2,1,0:T(8,128)(2,1)} %copy-done.12, bf16[8]{0:T(256)(128)(2,1)S(1)} %fusion.48, bf16[4,4,32,2560]{3,2,1,0:T(8,128)(2,1)S(1)} %get-tuple-element.38, bf16[4,4,32,2560]{3,2,1,0:T(8,128)(2,1)S(1)} %get-tuple-element.37), kind=kOutput, calls=%fused_computation.14 | convolution fusion | flops 18124636160 | bytes 47710224 | tf_op jit(solution)/shard_map/dot_general | solution.py:113
  104.7 4.3 %fusion.8 = bf16[4,2,216,768]{3,2,1,0:T(8,128)(2,1)} fusion(f32[4,2,2,216,2560]{4,3,2,1,0:T(8,128)} %bitcast.112, s32[]{:T(128)S(6)} %select_n.93), kind=kLoop, calls=%fused_computation.22 | loop fusion | bytes 5308420 | tf_op jit(solution)/shard_map/convert_element_type | solution.py:68
  109.1 5.2 %constant_dynamic-slice_fusion.2 = (bf16[4,2,1,216,896]{4,3,2,1,0:T(8,128)(2,1)S(1)}, bf16[4,2,1,216,896]{4,3,2,1,0:T(8,128)(2,1)S(1)}) fusion(f32[4,2,2,216,2560]{4,3,2,1,0:T(8,128)} %bitcast.113, s32[]{:T(128)S(6)} %select_n.93), kind=kLoop, calls=%fused_computation.124 | loop fusion | bytes 12386308 | tf_op jit(solution)/shard_map/dynamic_slice | solution.py:66
  114.3 2.0 copy.27
  120.2 9.9 %constant_dynamic-slice_fusion.3 = (f32[4,2,1,216,896]{4,3,2,1,0:T(8,128)}, f32[4,2,1,216,896]{4,3,2,1,0:T(8,128)}) fusion(f32[4,2,2,216,2560]{4,3,2,1,0:T(8,128)} %bitcast.114, s32[]{:T(128)S(6)} %select_n.92), kind=kLoop, calls=%fused_computation.125 | loop fusion | bytes 24772612 | tf_op jit(solution)/shard_map/dynamic_slice | solution.py:66
  131.9 58.2 %psum.7 = f32[2560]{0:T(1024)} all-reduce(f32[2560]{0:T(1024)S(1)} %convert_reduce_fusion), channel_id=1, replica_groups=mesh['dp'=4,'tile'=4,'seq'=2] {'dp','tile'}, use_global_device_ids=true, to_apply=%region_1.2 | all-reduce | flops 2560 | bytes 20480 | tf_op jit(solution)/shard_map/psum | solution.py:123
  190.1 2.2 pad_maximum_fusion
  192.4 3.3 bitcast_multiply_fusion
  195.6 4.0 %bitcast_add_fusion.2 = f32[4,2,216,768]{3,2,1,0:T(8,128)S(1)} fusion(bf16[4,2,216,768]{3,2,1,0:T(8,128)(2,1)} %collective-permute-done.17, f32[4,2,2,216,2560]{4,3,2,1,0:T(8,128)} %bitcast.116, s32[]{:T(128)S(6)} %select_n.92), kind=kLoop, calls=%fused_computation.10 | loop fusion | flops 2654208 | bytes 13271044 | tf_op jit(solution)/shard_map/add | solution.py:69
  200.9 2.6 collective-permute-start.19
  203.6 2.8 bitcast_add_fusion
  207.8 2.0 collective-permute-start.13
  209.9 2.6 bitcast_add_fusion.1
  212.5 2.6 copy-done.2
  217.5 23.9 %multiply_convert_fusion = bf16[8,4,32,2560]{3,2,1,0:T(8,128)(2,1)S(1)} fusion(bf16[8,4,32,3456]{3,2,1,0:T(8,128)(2,1)} %copy-done.12, bf16[3456,2560]{1,0:T(8,128)(2,1)} %all-gather.2.cloned.1.call-done, f32[8]{0:T(128)S(1)} %copy-done.16, f32[2560]{0:T(1024)S(1)} %convert_add_fusion), kind=kOutput, calls=%fused_computation.3 | convolution fusion | flops 18127257600 | bytes 30025760 | tf_op jit(solution)/shard_map/dot_general | solution.py:127
  241.4 2.3 copy-done.1
  244.9 27.2 %convolution_add_fusion = f32[1024,3456]{1,0:T(8,128)} fusion(bf16[1024,2560]{1,0:T(8,128)(2,1)} %bitcast_multiply_fusion, bf16[3456,2560]{1,0:T(8,128)(2,1)} %all-gather.2.cloned.1.call-done, f32[]{:T(128)} %bitcast.11), kind=kOutput, calls=%fused_computation.4 | convolution fusion | flops 18122932224 | bytes 37093380 | tf_op jit(solution)/shard_map/dot_general | solution.py:140
  274.0 2.8 broadcast_select_fusion.1
  280.2 6.7 %fusion.49 = (f32[8,4,31,128]{3,2,1,0:T(8,128)S(1)}, f32[8,4,31,128]{3,2,1,0:T(8,128)S(1)}, f32[8,4,31,128]{3,2,1,0:T(8,128)S(1)}, f32[8,4,31,128]{3,2,1,0:T(8,1...) fusion(f32[8,4,32,3456]{3,2,1,0:T(8,128)} %bitcast.122), kind=kLoop, calls=%fused_computation.128 | loop fusion | bytes 18284544 | tf_op jit(solution)/shard_map/slice | solution.py:161
  289.5 3.0 collective-permute-start.16
  292.5 3.5 fusion.50
  297.7 6.8 %collective-permute-start.4 = (f32[8,1,32,128]{3,2,1,0:T(8,128)S(1)}, f32[8,1,32,128]{3,2,1,0:T(8,128)S(1)}, u32[]{:S(2)}, u32[]{:S(2)}) collective-permute-start(f32[8,1,32,128]{3,2,1,0:T(8,128)S(1)} %get-tuple-element.48), channel_id=1, source_target_pairs={{0,2},{2,4},{4,6},{1,3},{3,5},{5,7},{8,10},{10,12},{12,14},{9,11},... | collective-permute-start | bytes 393224 | tf_op jit(solution)/shard_map/ppermute | solution.py:41
  308.5 5.2 %collective-permute-done.5 = f32[8,1,32,128]{3,2,1,0:T(8,128)S(1)} collective-permute-done((f32[8,1,32,128]{3,2,1,0:T(8,128)S(1)}, f32[8,1,32,128]{3,2,1,0:T(8,128)S(1)}, u32[]{:S(2)}, u32[]{:S(2)}) %collective-permute-start.5) | collective-permute-done | bytes 131104 | tf_op jit(solution)/shard_map/ppermute | solution.py:41
  319.6 27.6 %collective-permute-done.15 = bf16[216,896]{1,0:T(8,128)(2,1)S(1)} collective-permute-done((bf16[216,896]{1,0:T(8,128)(2,1)S(1)}, bf16[216,896]{1,0:T(8,128)(2,1)S(1)}, u32[]{:S(2)}, u32[]{:S(2)}) %collective-permute-start.15) | collective-permute-done | bytes 387104 | tf_op jit(solution)/shard_map/ppermute | solution.py:16
  347.7 15.6 %collective-permute-done.10 = bf16[216,896]{1,0:T(8,128)(2,1)S(1)} collective-permute-done((bf16[216,896]{1,0:T(8,128)(2,1)S(1)}, bf16[216,896]{1,0:T(8,128)(2,1)S(1)}, u32[]{:S(2)}, u32[]{:S(2)}) %collective-permute-start.10) | collective-permute-done | bytes 387104 | tf_op jit(solution)/shard_map/ppermute | solution.py:16
  366.8 3.0 maximum_bitcast_fusion
  (147 shorter events, 39.8 us)
Async XLA Ops:
  7.2 210.3 %all-gather.2.cloned.1.call-start = ((), (), s32[]{:S(2)}) async-start(), calls=%async_computation | async-start | bytes 18800640 | tf_op jit(solution)/shard_map/all_gather | solution.py:125
  9.7 12.0 %collective-permute-start = (bf16[8,1,32,128]{3,2,1,0:T(8,128)(2,1)S(1)}, bf16[8,1,32,128]{3,2,1,0:T(8,128)(2,1)S(1)}, u32[]{:S(2)}, u32[]{:S(2)}) collective-permute-start(bf16[8,1,32,128]{3,2,1,0:T(8,128)(2,1)S(1)} %get-tuple-element.53), channel_id=1, source_target_pairs={{0,2},{2,4},{4,6},{1,3},{3,5},{5,7},{8,10},{10,12},{12,14},{9,11},... | collective-permute-start | bytes 196616 | tf_op jit(solution)/shard_map/ppermute | solution.py:41
  14.2 7.4 %collective-permute-start.1 = (bf16[8,1,32,128]{3,2,1,0:T(8,128)(2,1)S(1)}, bf16[8,1,32,128]{3,2,1,0:T(8,128)(2,1)S(1)}, u32[]{:S(2)}, u32[]{:S(2)}) collective-permute-start(bf16[8,1,32,128]{3,2,1,0:T(8,128)(2,1)S(1)} %get-tuple-element.54), channel_id=1, source_target_pairs={{2,0},{4,2},{6,4},{3,1},{5,3},{7,5},{10,8},{12,10},{14,12},{11,9},... | collective-permute-start | bytes 196616 | tf_op jit(solution)/shard_map/ppermute | solution.py:41
  19.0 57.1 %collective-permute-start.2 = (bf16[4,4,32,2560]{3,2,1,0:T(8,128)(2,1)S(1)}, bf16[4,4,32,2560]{3,2,1,0:T(8,128)(2,1)}, u32[]{:S(2)}, u32[]{:S(2)}) collective-permute-start(bf16[4,4,32,2560]{3,2,1,0:T(8,128)(2,1)S(1)} %broadcast_select_fusion.3), channel_id=1, source_target_pairs={{0,1},{1,0},{2,3},{3,2},{4,5},{5,4},{6,7},{7,6},{8,9},{9,8},{10,11... | collective-permute-start | bytes 7864328 | tf_op jit(solution)/shard_map/ppermute | solution.py:16
  22.4 53.7 %slice-start.4 = ((s8[5242880]{0:T(1024)(128)(4,1)}), s8[4194304]{0:T(1024)(128)(4,1)S(1)}, s32[]{:S(2)}) async-start(s8[5242880]{0:T(1024)(128)(4,1)} %bitcast.107), calls=%async_computation.5 | async-start | bytes 8388608
  23.0 53.1 %slice-start.5 = ((s8[5242880]{0:T(1024)(128)(4,1)}), s8[1048576]{0:T(1024)(128)(4,1)S(1)}, s32[]{:S(2)}) async-start(s8[5242880]{0:T(1024)(128)(4,1)} %bitcast.107), calls=%async_computation.6 | async-start | bytes 2097152
  78.4 40.3 %copy-start = (bf16[4,4,32,2560]{3,2,1,0:T(8,128)(2,1)}, bf16[4,4,32,2560]{3,2,1,0:T(8,128)(2,1)S(1)}, u32[]{:S(2)}) copy-start(bf16[4,4,32,2560]{3,2,1,0:T(8,128)(2,1)S(1)} %get-tuple-element.38) | copy-start | bytes 7864324
  109.0 86.6 %collective-permute-start.17 = (bf16[4,2,216,768]{3,2,1,0:T(8,128)(2,1)}, bf16[4,2,216,768]{3,2,1,0:T(8,128)(2,1)}, u32[]{:S(2)}, u32[]{:S(2)}) collective-permute-start(bf16[4,2,216,768]{3,2,1,0:T(8,128)(2,1)} %fusion.8), channel_id=1, source_target_pairs={{0,2},{2,0},{4,6},{6,4},{1,3},{3,1},{5,7},{7,5},{8,10},{10,8},{12,... | collective-permute-start | bytes 7962632 | tf_op jit(solution)/shard_map/ppermute | solution.py:16
  118.2 85.3 %collective-permute-start.12 = (bf16[4,2,216,896]{3,2,0,1:T(8,128)(2,1)}, bf16[4,2,216,896]{3,2,0,1:T(8,128)(2,1)}, u32[]{:S(2)}, u32[]{:S(2)}) collective-permute-start(bf16[4,2,216,896]{3,2,0,1:T(8,128)(2,1)} %bitcast.99), channel_id=1, source_target_pairs={{0,2},{2,0},{4,6},{6,4},{1,3},{3,1},{5,7},{7,5},{8,10},{10,8},{12,... | collective-permute-start | bytes 9289736 | tf_op jit(solution)/shard_map/ppermute | solution.py:16
  118.7 91.1 %collective-permute-start.7 = (bf16[4,2,216,896]{3,2,0,1:T(8,128)(2,1)}, bf16[4,2,216,896]{3,2,0,1:T(8,128)(2,1)}, u32[]{:S(2)}, u32[]{:S(2)}) collective-permute-start(bf16[4,2,216,896]{3,2,0,1:T(8,128)(2,1)} %bitcast.98), channel_id=1, source_target_pairs={{0,2},{2,0},{4,6},{6,4},{1,3},{3,1},{5,7},{7,5},{8,10},{10,8},{12,... | collective-permute-start | bytes 9289736 | tf_op jit(solution)/shard_map/ppermute | solution.py:16
  120.2 70.0 %copy-start.14 = (bf16[2560]{0:T(1024)(128)(2,1)S(1)}, bf16[2560]{0:T(1024)(128)(2,1)}, u32[]{:S(2)}) copy-start(bf16[2560]{0:T(1024)(128)(2,1)} %param.8) | copy-start | bytes 15364
  192.4 11.2 %slice-start.2 = ((s8[6193152]{0:T(1024)(128)(4,1)}), s8[4194304]{0:T(1024)(128)(4,1)S(1)}, s32[]{:S(2)}) async-start(s8[6193152]{0:T(1024)(128)(4,1)} %bitcast.104), calls=%async_computation.3 | async-start | bytes 8388608
  200.9 75.9 %collective-permute-start.18 = (bf16[2,216,768]{2,1,0:T(8,128)(2,1)}, bf16[2,216,768]{2,1,0:T(8,128)(2,1)S(1)}, u32[]{:S(2)}, u32[]{:S(2)}) collective-permute-start(bf16[2,216,768]{2,1,0:T(8,128)(2,1)} %get-tuple-element.39), channel_id=1, source_target_pairs={{0,8},{8,0},{16,24},{24,16},{1,9},{9,1},{17,25},{25,17},{2,10},{10... | collective-permute-start | bytes 1990664 | tf_op jit(solution)/shard_map/ppermute | solution.py:16
  200.9 77.3 %collective-permute-start.20 = (bf16[2,216,768]{2,1,0:T(8,128)(2,1)S(1)}, bf16[2,216,768]{2,1,0:T(8,128)(2,1)S(1)}, u32[]{:S(2)}, u32[]{:S(2)}) collective-permute-start(bf16[2,216,768]{2,1,0:T(8,128)(2,1)S(1)} %get-tuple-element.40), channel_id=1, source_target_pairs={{0,24},{8,16},{16,8},{24,0},{1,25},{9,17},{17,9},{25,1},{2,26},{10... | collective-permute-start | bytes 1990664 | tf_op jit(solution)/shard_map/ppermute | solution.py:16
  200.9 77.3 %collective-permute-start.19 = (bf16[2,216,768]{2,1,0:T(8,128)(2,1)S(1)}, bf16[2,216,768]{2,1,0:T(8,128)(2,1)S(1)}, u32[]{:S(2)}, u32[]{:S(2)}) collective-permute-start(bf16[2,216,768]{2,1,0:T(8,128)(2,1)S(1)} %get-tuple-element.41), channel_id=1, source_target_pairs={{0,16},{8,24},{16,0},{24,8},{1,17},{9,25},{17,1},{25,9},{2,18},{10... | collective-permute-start | bytes 1990664 | tf_op jit(solution)/shard_map/ppermute | solution.py:16
  207.8 79.2 %collective-permute-start.13 = (bf16[4,216,896]{2,1,0:T(8,128)(2,1)}, bf16[4,216,896]{2,1,0:T(8,128)(2,1)}, u32[]{:S(2)}, u32[]{:S(2)}) collective-permute-start(bf16[4,216,896]{2,1,0:T(8,128)(2,1)} %fusion.11), channel_id=1, source_target_pairs={{0,4},{2,6},{4,0},{6,2},{1,5},{3,7},{5,1},{7,3},{8,12},{10,14},{12... | collective-permute-start | bytes 4644872 | tf_op jit(solution)/shard_map/ppermute | solution.py:16
  216.4 81.3 %collective-permute-start.8 = (bf16[4,216,896]{2,1,0:T(8,128)(2,1)}, bf16[4,216,896]{2,1,0:T(8,128)(2,1)}, u32[]{:S(2)}, u32[]{:S(2)}) collective-permute-start(bf16[4,216,896]{2,1,0:T(8,128)(2,1)} %fusion.10), channel_id=1, source_target_pairs={{0,4},{2,6},{4,0},{6,2},{1,5},{3,7},{5,1},{7,3},{8,12},{10,14},{12... | collective-permute-start | bytes 4644872 | tf_op jit(solution)/shard_map/ppermute | solution.py:16
  276.8 89.3 %collective-permute-start.3 = (bf16[4,4,32,2560]{3,2,1,0:T(8,128)(2,1)S(1)}, bf16[4,4,32,2560]{3,2,1,0:T(8,128)(2,1)S(1)}, u32[]{:S(2)}, u32[]{:S(2)}) collective-permute-start(bf16[4,4,32,2560]{3,2,1,0:T(8,128)(2,1)S(1)} %broadcast_select_fusion.1), channel_id=1, source_target_pairs={{0,1},{1,0},{2,3},{3,2},{4,5},{5,4},{6,7},{7,6},{8,9},{9,8},{10,11... | collective-permute-start | bytes 7864328 | tf_op jit(solution)/shard_map/ppermute | solution.py:16
  279.8 35.8 %collective-permute-start.21 = (bf16[216,768]{1,0:T(8,128)(2,1)S(1)}, bf16[216,768]{1,0:T(8,128)(2,1)}, u32[]{:S(2)}, u32[]{:S(2)}) collective-permute-start(bf16[216,768]{1,0:T(8,128)(2,1)S(1)} %fusion.46), channel_id=1, source_target_pairs={{0,4},{2,6},{4,0},{6,2},{1,5},{3,7},{5,1},{7,3},{8,12},{10,14},{12... | collective-permute-start | bytes 995336 | tf_op jit(solution)/shard_map/ppermute | solution.py:16
  289.1 28.1 %collective-permute-start.14 = (bf16[216,896]{1,0:T(8,128)(2,1)S(1)}, bf16[216,896]{1,0:T(8,128)(2,1)S(1)}, u32[]{:S(2)}, u32[]{:S(2)}) collective-permute-start(bf16[216,896]{1,0:T(8,128)(2,1)S(1)} %get-tuple-element.45), channel_id=1, source_target_pairs={{0,8},{8,0},{16,24},{24,16},{1,9},{9,1},{17,25},{25,17},{2,10},{10... | collective-permute-start | bytes 1161224 | tf_op jit(solution)/shard_map/ppermute | solution.py:16
  289.5 28.0 %collective-permute-start.16 = (bf16[216,896]{1,0:T(8,128)(2,1)S(1)}, bf16[216,896]{1,0:T(8,128)(2,1)S(1)}, u32[]{:S(2)}, u32[]{:S(2)}) collective-permute-start(bf16[216,896]{1,0:T(8,128)(2,1)S(1)} %get-tuple-element.46), channel_id=1, source_target_pairs={{0,24},{8,16},{16,8},{24,0},{1,25},{9,17},{17,9},{25,1},{2,26},{10... | collective-permute-start | bytes 1161224 | tf_op jit(solution)/shard_map/ppermute | solution.py:16
  297.7 17.8 %copy-start.17 = (f32[4]{0:T(128)S(1)}, f32[4]{0:T(128)}, u32[]{:S(2)}) copy-start(f32[4]{0:T(128)} %pad.128.clone) | copy-start | bytes 52
  297.7 8.7 %collective-permute-start.4 = (f32[8,1,32,128]{3,2,1,0:T(8,128)S(1)}, f32[8,1,32,128]{3,2,1,0:T(8,128)S(1)}, u32[]{:S(2)}, u32[]{:S(2)}) collective-permute-start(f32[8,1,32,128]{3,2,1,0:T(8,128)S(1)} %get-tuple-element.48), channel_id=1, source_target_pairs={{0,2},{2,4},{4,6},{1,3},{3,5},{5,7},{8,10},{10,12},{12,14},{9,11},... | collective-permute-start | bytes 393224 | tf_op jit(solution)/shard_map/ppermute | solution.py:41
  306.4 7.3 %collective-permute-start.5 = (f32[8,1,32,128]{3,2,1,0:T(8,128)S(1)}, f32[8,1,32,128]{3,2,1,0:T(8,128)S(1)}, u32[]{:S(2)}, u32[]{:S(2)}) collective-permute-start(f32[8,1,32,128]{3,2,1,0:T(8,128)S(1)} %get-tuple-element.49), channel_id=1, source_target_pairs={{2,0},{4,2},{6,4},{3,1},{5,3},{7,5},{10,8},{12,10},{14,12},{11,9},... | collective-permute-start | bytes 393224 | tf_op jit(solution)/shard_map/ppermute | solution.py:41
  313.7 33.5 %collective-permute-start.15 = (bf16[216,896]{1,0:T(8,128)(2,1)S(1)}, bf16[216,896]{1,0:T(8,128)(2,1)S(1)}, u32[]{:S(2)}, u32[]{:S(2)}) collective-permute-start(bf16[216,896]{1,0:T(8,128)(2,1)S(1)} %get-tuple-element.47), channel_id=1, source_target_pairs={{0,16},{8,24},{16,0},{24,8},{1,17},{9,25},{17,1},{25,9},{2,18},{10... | collective-permute-start | bytes 1161224 | tf_op jit(solution)/shard_map/ppermute | solution.py:16
  315.5 50.7 %slice-start.6 = ((s8[5242880]{0:T(1024)(128)(4,1)}), s8[4194304]{0:T(1024)(128)(4,1)S(1)}, s32[]{:S(2)}) async-start(s8[5242880]{0:T(1024)(128)(4,1)} %bitcast.110), calls=%async_computation.7 | async-start | bytes 8388608
  315.6 32.0 %collective-permute-start.9 = (bf16[216,896]{1,0:T(8,128)(2,1)S(1)}, bf16[216,896]{1,0:T(8,128)(2,1)S(1)}, u32[]{:S(2)}, u32[]{:S(2)}) collective-permute-start(bf16[216,896]{1,0:T(8,128)(2,1)S(1)} %get-tuple-element.42), channel_id=1, source_target_pairs={{0,8},{8,0},{16,24},{24,16},{1,9},{9,1},{17,25},{25,17},{2,10},{10... | collective-permute-start | bytes 1161224 | tf_op jit(solution)/shard_map/ppermute | solution.py:16
  317.2 30.4 %collective-permute-start.11 = (bf16[216,896]{1,0:T(8,128)(2,1)S(1)}, bf16[216,896]{1,0:T(8,128)(2,1)S(1)}, u32[]{:S(2)}, u32[]{:S(2)}) collective-permute-start(bf16[216,896]{1,0:T(8,128)(2,1)S(1)} %get-tuple-element.43), channel_id=1, source_target_pairs={{0,24},{8,16},{16,8},{24,0},{1,25},{9,17},{17,9},{25,1},{2,26},{10... | collective-permute-start | bytes 1161224 | tf_op jit(solution)/shard_map/ppermute | solution.py:16
  317.5 45.8 %collective-permute-start.10 = (bf16[216,896]{1,0:T(8,128)(2,1)S(1)}, bf16[216,896]{1,0:T(8,128)(2,1)S(1)}, u32[]{:S(2)}, u32[]{:S(2)}) collective-permute-start(bf16[216,896]{1,0:T(8,128)(2,1)S(1)} %get-tuple-element.44), channel_id=1, source_target_pairs={{0,16},{8,24},{16,0},{24,8},{1,17},{9,25},{17,1},{25,9},{2,18},{10... | collective-permute-start | bytes 1161224 | tf_op jit(solution)/shard_map/ppermute | solution.py:16
  347.2 17.9 %collective-permute-start.6 = (f32[8,4,32,128]{3,2,1,0:T(8,128)S(1)}, f32[8,4,32,128]{3,2,1,0:T(8,128)S(1)}, u32[]{:S(2)}, u32[]{:S(2)}) collective-permute-start(f32[8,4,32,128]{3,2,1,0:T(8,128)S(1)} %slice_add_fusion), channel_id=1, source_target_pairs={{0,1},{1,0},{2,3},{3,2},{4,5},{5,4},{6,7},{7,6},{8,9},{9,8},{10,11... | collective-permute-start | bytes 1572872 | tf_op jit(solution)/shard_map/ppermute | solution.py:16
  347.6 17.5 %copy-start.11 = (bf16[1,8,4,32,128]{4,3,2,1,0:T(8,128)(2,1)S(1)}, bf16[1,8,4,32,128]{4,3,2,1,0:T(8,128)(2,1)}, u32[]{:S(2)}) copy-start(bf16[1,8,4,32,128]{4,3,2,1,0:T(8,128)(2,1)} %param.5) | copy-start | bytes 786436
  347.6 18.5 %slice-start.7 = ((s8[5242880]{0:T(1024)(128)(4,1)}), s8[1048576]{0:T(1024)(128)(4,1)S(1)}, s32[]{:S(2)}) async-start(s8[5242880]{0:T(1024)(128)(4,1)} %bitcast.110), calls=%async_computation.8 | async-start | bytes 2097152
  (21 other events, 114.1 us)
Sparse Core Ops, SparseCore 0:
  9.6 95.8 all-gather.1

commit v4 on v3

--- a/solution.py
+++ b/solution.py
@@ -118,10 +118,10 @@
     first = (units - last) // 2
     widths = [128 * first, 128 * (units - last - first), 128 * last]
     starts = [0, widths[0], widths[0] + widths[1]]
-    partials = [pair_rows(weight_term, c, w) for c, w in zip(starts, widths)]
-    moving = [scatter_tile(partials[0]), scatter_dp(partials[2]), scatter_tile(partials[1])]
-    grad_bias = lax.psum(jnp.sum(flat_grad, axis=0, dtype=jnp.float32), ("dp", "tile"))
-
+    grad_bias = sum_over(jnp.sum(flat_grad, axis=0, dtype=jnp.float32), ("dp", "tile"))
+    settled = 0.0 * grad_bias[0]
+    partials = [pair_rows(weight_term, c, w) + settled for c, w in zip(starts, widths)]
+    moving = [scatter_tile(partials[0]), scatter_dp(partials[2])]
     full_weight = lax.all_gather(weight, ("dp", "tile"), axis=0, tiled=True)
     bias_vals = bias.astype(jnp.float32) + 0.0 * weight_term[0, 0]
     output = jnp.dot(columns, full_weight, preferred_element_type=jnp.float32)
@@ -137,16 +137,19 @@
     )
 
     after = 0.0 * tokens[0, 0, 0, 0].astype(jnp.float32)
+    added = scatter_end(moving[0], after)
+    then = 0.0 * added[0, 0, 0]
+    moving = [scatter_dp(added), moving[1], scatter_tile(partials[1] + after)]
     spread = lax.dot_general(
         flat_grad, full_weight, (((1,), (1,)), ((), ())), preferred_element_type=jnp.float32
     )
+    spread = (spread + then).reshape(frame_count, row_count, col_count, 27 * chan_count)
+    late = 0.0 * spread[0, 0, 0, 0]
     moving = [
-        scatter_dp(scatter_end(moving[0], after)),
-        scatter_tile(scatter_end(moving[1], after)),
-        scatter_dp(scatter_end(moving[2], after)),
+        moving[0],
+        scatter_tile(scatter_end(moving[1], then)),
+        scatter_dp(scatter_end(moving[2], then)),
     ]
-    spread = (spread + after).reshape(frame_count, row_count, col_count, 27 * chan_count)
-    late = 0.0 * spread[0, 0, 0, 0]
     ended = [scatter_end(terms, late) for terms in moving]
     grad_weight = jnp.concatenate([ended[0], ended[2], ended[1]], axis=1)
     total = jnp.zeros((frame_count, row_count + 2, col_count, chan_count), jnp.float32)

time: 377 us -> 347 us (0.920)
  blocking collectives: 58.2 us -> 0 us
  waiting for transfers between devices: 98.7 us -> 124 us
  starting transfers between devices: 32.7 us -> 38 us
  local copies, waits for them, and re-layouts: 48.2 us -> 43.9 us
    psum x1 -> x0, blocking collectives: 58.2 us -> none  [shards(): lax.psum(jnp.sum(flat_grad, axis=0, dtype=jnp.float32), ('dp', 'tile'))]
    ppermute x2, waiting for transfers between devices: 0.07 us -> 17.8 us  [neighbours(): lax.ppermute(high_row, axis, forward)]
    ppermute x18 -> x22, waiting for transfers between devices: 92.8 us -> 103 us  [swap(): return lax.ppermute(value, axis, [(i, i ^ distance) for i in range(count)])]
    ppermute x18 -> x22, starting transfers between devices: 17.5 us -> 22.9 us  [swap(): return lax.ppermute(value, axis, [(i, i ^ distance) for i in range(count)])]
    unnamed x70 -> x54, local copies, waits for them, and re-layouts: 12.9 us -> 10.6 us
    add x3 -> x7, other arithmetic: 9.41 us -> 9.1 us  [the longest x2 6.41 us: shards(): pair_rows(weight_term, c, w) + settled]
  transfers between devices with their start and end apart: 23 -> 27, of which waited for: 5 -> 8; matrix products, arithmetic and copies ran while one was open for 42% -> 45% of each run, Pallas kernels for 0% -> 0%
where the time goes in v4:
time: 347 us
  waiting for transfers between devices  124 us (36%)
  matrix products  76.6 us (22%)
  other arithmetic  45.4 us (13%)
  local copies, waits for them, and re-layouts  43.9 us (13%)
  starting transfers between devices  38 us (11%)
  between operations  18.6 us (5%)
    ppermute x22, waiting for transfers between devices, swap(): return lax.ppermute(value, axis, [(i, i ^ distance) for i in range(count)])  103 us
    dot_general x1, matrix products, shards(): lax.dot_general(flat_grad, full_weight, (((1,), (1,)), ((), ())), preferr...  27.5 us
    dot_general x1, matrix products, shards(): lax.dot_general(columns, flat_grad, (((0,), (0,)), ((), ())), preferred_e...  25.3 us
    dot_general x1, matrix products, shards(): output = jnp.dot(columns, full_weight, preferred_element_type=jnp.float32)  23.9 us
    ppermute x22, starting transfers between devices, swap(): return lax.ppermute(value, axis, [(i, i ^ distance) for i in range(count)])  22.9 us
    ppermute x2, waiting for transfers between devices, neighbours(): lax.ppermute(high_row, axis, forward)  17.8 us
    dynamic_slice x2, local copies, waits for them, and re-layouts, rows_of(): return lax.dynamic_slice(value, (0, 0, parity, 0, start), sizes)[:, :, 0]  14.8 us
    ppermute x2, starting transfers between devices, neighbours(): lax.ppermute(high_row, axis, forward)  10.9 us
  transfers between devices with their start and end apart: 27, of which 8 were waited for; matrix products, arithmetic and copies ran while one was open for 45% of the time, Pallas kernels for 0%

profile of v4, /device:TPU:1, one launch (start us, length us, event | category | flops | bytes accessed | tf_op | source)
XLA Modules:
  0.0 346.6 jit_solution(15276084620497360120)
XLA Ops:
  9.7 4.5 %collective-permute-start = (bf16[8,1,32,128]{3,2,1,0:T(8,128)(2,1)S(1)}, bf16[8,1,32,128]{3,2,1,0:T(8,128)(2,1)S(1)}, u32[]{:S(2)}, u32[]{:S(2)}) collective-permute-start(bf16[8,1,32,128]{3,2,1,0:T(8,128)(2,1)S(1)} %get-tuple-element.53), channel_id=1, source_target_pairs={{0,2},{2,4},{4,6},{1,3},{3,5},{5,7},{8,10},{10,12},{12,14},{9,11},... | collective-permute-start | bytes 196616 | tf_op jit(solution)/shard_map/ppermute | solution.py:41
  16.2 2.8 broadcast_select_fusion.3
  23.8 52.3 %collective-permute-done.2 = bf16[4,4,32,2560]{3,2,1,0:T(8,128)(2,1)} collective-permute-done((bf16[4,4,32,2560]{3,2,1,0:T(8,128)(2,1)S(1)}, bf16[4,4,32,2560]{3,2,1,0:T(8,128)(2,1)}, u32[]{:S(2)}, u32[]{:S(2)}) %collective-permute-start.2) | collective-permute-done | bytes 2621472 | tf_op jit(solution)/shard_map/ppermute | solution.py:16
  76.1 2.0 broadcast_select_fusion.6
  78.1 25.3 %fusion.8 = f32[3456,2560,1,1]{1,0,3,2:T(8,128)} fusion(bf16[8,4,32,3456]{3,2,1,0:T(8,128)(2,1)} %copy-done.9, bf16[8]{0:T(256)(128)(2,1)S(1)} %fusion.52, bf16[4,4,32,2560]{3,2,1,0:T(8,128)(2,1)S(1)} %get-tuple-element.38, bf16[4,4,32,2560]{3,2,1,0:T(8,128)(2,1)S(1)} %get-tuple-element.37), kind=kOutput, calls=%fused_computation.18 | convolution fusion | flops 18124636160 | bytes 47710224 | tf_op jit(solution)/shard_map/dot_general | solution.py:113
  103.4 4.4 %fusion.12 = bf16[4,2,216,768]{3,2,1,0:T(8,128)(2,1)} fusion(f32[4,2,2,216,2560]{4,3,2,1,0:T(8,128)} %bitcast.120, s32[]{:T(128)S(6)} %select_n.93), kind=kLoop, calls=%fused_computation.26 | loop fusion | bytes 5308420 | tf_op jit(solution)/shard_map/convert_element_type | solution.py:68
  107.8 6.9 %constant_dynamic-slice_fusion = (bf16[4,2,1,216,896]{4,3,2,1,0:T(8,128)(2,1)}, bf16[4,2,1,216,896]{4,3,2,1,0:T(8,128)(2,1)S(1)}) fusion(f32[4,2,2,216,2560]{4,3,2,1,0:T(8,128)} %bitcast.121, s32[]{:T(128)S(6)} %select_n.93), kind=kLoop, calls=%fused_computation.126 | loop fusion | bytes 12386308 | tf_op jit(solution)/shard_map/dynamic_slice | solution.py:66
  114.7 2.0 copy.27
  120.6 2.8 pad_maximum_fusion
  123.4 2.3 collective-permute-start.6
  125.7 8.0 %constant_dynamic-slice_fusion.1 = (f32[4,2,1,216,896]{4,3,2,1,0:T(8,128)}, f32[4,2,1,216,896]{4,3,2,1,0:T(8,128)S(1)}) fusion(f32[4,2,2,216,2560]{4,3,2,1,0:T(8,128)} %bitcast.122, s32[]{:T(128)S(6)} %select_n.92), kind=kLoop, calls=%fused_computation.127 | loop fusion | bytes 24772612 | tf_op jit(solution)/shard_map/dynamic_slice | solution.py:66
  133.7 3.8 %copy.28 = bf16[4,2,1,216,896]{4,3,0,1,2:T(8,128)(2,1)} copy(bf16[4,2,1,216,896]{4,3,2,1,0:T(8,128)(2,1)} %get-tuple-element.4) | data formatting | bytes 6193152
  138.1 5.3 %bitcast_multiply_fusion = bf16[1024,2560]{1,0:T(8,128)(2,1)} fusion(bf16[8,4,32,2560]{3,2,1,0:T(8,128)(2,1)} %pad_maximum_fusion, bf16[1024]{0:T(1024)(128)(2,1)S(1)} %copy-done.11), kind=kLoop, calls=%fused_computation.17 | loop fusion | flops 2621440 | bytes 10487808 | tf_op jit(solution)/shard_map/mul | solution.py:99
  145.2 2.0 collective-permute-start.8
  149.5 3.9 %fusion.7 = f32[4,2,216,768]{3,2,1,0:T(8,128)S(1)} fusion(bf16[4,2,216,768]{3,2,1,0:T(8,128)(2,1)} %collective-permute-done.21, f32[4,2,2,216,2560]{4,3,2,1,0:T(8,128)} %bitcast.124, s32[]{:T(128)S(6)} %select_n.92, f32[]{:T(128)} %bitcast.16), kind=kLoop, calls=%fused_computation.14 | loop fusion | flops 3981312 | bytes 13271048 | tf_op jit(solution)/shard_map/add | solution.py:123
  157.6 2.5 fusion.4
  160.1 2.6 copy-done.1
  164.4 23.9 %multiply_convert_fusion = bf16[8,4,32,2560]{3,2,1,0:T(8,128)(2,1)S(1)} fusion(bf16[8,4,32,3456]{3,2,1,0:T(8,128)(2,1)} %copy-done.9, bf16[3456,2560]{1,0:T(8,128)(2,1)} %all-gather.2.cloned.1.call-done, f32[8]{0:T(128)S(1)} %copy-done.14, f32[2560]{0:T(1024)S(1)} %convert_add_fusion), kind=kOutput, calls=%fused_computation.3 | convolution fusion | flops 18127257600 | bytes 30025760 | tf_op jit(solution)/shard_map/dot_general | solution.py:127
  191.6 4.5 %collective-permute-done.9 = bf16[4,216,896]{2,1,0:T(8,128)(2,1)S(1)} collective-permute-done((bf16[4,216,896]{2,1,0:T(8,128)(2,1)S(1)}, bf16[4,216,896]{2,1,0:T(8,128)(2,1)S(1)}, u32[]{:S(2)}, u32[]{:S(2)}) %collective-permute-start.9) | collective-permute-done | bytes 1548320 | tf_op jit(solution)/shard_map/ppermute | solution.py:16
  200.3 27.5 %convolution_add_fusion = f32[1024,3456]{1,0:T(8,128)} fusion(bf16[1024,2560]{1,0:T(8,128)(2,1)} %bitcast_multiply_fusion, bf16[3456,2560]{1,0:T(8,128)(2,1)} %all-gather.2.cloned.1.call-done, f32[]{:T(128)} %bitcast.20), kind=kOutput, calls=%fused_computation.4 | convolution fusion | flops 18122932224 | bytes 37093380 | tf_op jit(solution)/shard_map/dot_general | solution.py:143
  229.7 2.4 fusion.17
  233.3 6.0 %fusion.53 = (f32[8,4,31,128]{3,2,1,0:T(8,128)S(1)}, f32[8,4,31,128]{3,2,1,0:T(8,128)S(1)}, f32[8,4,31,128]{3,2,1,0:T(8,128)S(1)}, f32[8,4,31,128]{3,2,1,0:T(8,1...) fusion(f32[8,4,32,3456]{3,2,1,0:T(8,128)} %bitcast.126), kind=kLoop, calls=%fused_computation.132 | loop fusion | bytes 18284544 | tf_op jit(solution)/shard_map/slice | solution.py:164
  239.4 2.7 fusion.3
  243.5 3.4 fusion.54
  248.5 6.4 %collective-permute-start.10 = (f32[8,1,32,128]{3,2,1,0:T(8,128)S(1)}, f32[8,1,32,128]{3,2,1,0:T(8,128)S(1)}, u32[]{:S(2)}, u32[]{:S(2)}) collective-permute-start(f32[8,1,32,128]{3,2,1,0:T(8,128)S(1)} %get-tuple-element.48), channel_id=1, source_target_pairs={{0,2},{2,4},{4,6},{1,3},{3,5},{5,7},{8,10},{10,12},{12,14},{9,11},... | collective-permute-start | bytes 393224 | tf_op jit(solution)/shard_map/ppermute | solution.py:41
  255.0 2.2 collective-permute-start.11
  257.4 17.8 %collective-permute-done.10 = f32[8,1,32,128]{3,2,1,0:T(8,128)S(1)} collective-permute-done((f32[8,1,32,128]{3,2,1,0:T(8,128)S(1)}, f32[8,1,32,128]{3,2,1,0:T(8,128)S(1)}, u32[]{:S(2)}, u32[]{:S(2)}) %collective-permute-start.10) | collective-permute-done | bytes 131104 | tf_op jit(solution)/shard_map/ppermute | solution.py:41
  276.8 2.6 collective-permute-done.11
  286.0 5.2 %collective-permute-done.15 = bf16[216,896]{1,0:T(8,128)(2,1)S(1)} collective-permute-done((bf16[216,896]{1,0:T(8,128)(2,1)S(1)}, bf16[216,896]{1,0:T(8,128)(2,1)S(1)}, u32[]{:S(2)}, u32[]{:S(2)}) %collective-permute-start.15) | collective-permute-done | bytes 387104 | tf_op jit(solution)/shard_map/ppermute | solution.py:16
  291.7 28.1 %collective-permute-done.14 = bf16[216,896]{1,0:T(8,128)(2,1)S(1)} collective-permute-done((bf16[216,896]{1,0:T(8,128)(2,1)S(1)}, bf16[216,896]{1,0:T(8,128)(2,1)S(1)}, u32[]{:S(2)}, u32[]{:S(2)}) %collective-permute-start.14) | collective-permute-done | bytes 387104 | tf_op jit(solution)/shard_map/ppermute | solution.py:16
  321.1 11.8 %collective-permute-done.19 = bf16[216,896]{1,0:T(8,128)(2,1)S(1)} collective-permute-done((bf16[216,896]{1,0:T(8,128)(2,1)S(1)}, bf16[216,896]{1,0:T(8,128)(2,1)S(1)}, u32[]{:S(2)}, u32[]{:S(2)}) %collective-permute-start.19) | collective-permute-done | bytes 387104 | tf_op jit(solution)/shard_map/ppermute | solution.py:16
  336.7 3.0 maximum_bitcast_fusion
  (141 shorter events, 47.2 us)
Async XLA Ops:
  7.2 157.2 %all-gather.2.cloned.1.call-start = ((), (), s32[]{:S(2)}) async-start(), calls=%async_computation | async-start | bytes 18800640 | tf_op jit(solution)/shard_map/all_gather | solution.py:125
  9.7 12.0 %collective-permute-start = (bf16[8,1,32,128]{3,2,1,0:T(8,128)(2,1)S(1)}, bf16[8,1,32,128]{3,2,1,0:T(8,128)(2,1)S(1)}, u32[]{:S(2)}, u32[]{:S(2)}) collective-permute-start(bf16[8,1,32,128]{3,2,1,0:T(8,128)(2,1)S(1)} %get-tuple-element.53), channel_id=1, source_target_pairs={{0,2},{2,4},{4,6},{1,3},{3,5},{5,7},{8,10},{10,12},{12,14},{9,11},... | collective-permute-start | bytes 196616 | tf_op jit(solution)/shard_map/ppermute | solution.py:41
  14.2 7.4 %collective-permute-start.1 = (bf16[8,1,32,128]{3,2,1,0:T(8,128)(2,1)S(1)}, bf16[8,1,32,128]{3,2,1,0:T(8,128)(2,1)S(1)}, u32[]{:S(2)}, u32[]{:S(2)}) collective-permute-start(bf16[8,1,32,128]{3,2,1,0:T(8,128)(2,1)S(1)} %get-tuple-element.54), channel_id=1, source_target_pairs={{2,0},{4,2},{6,4},{3,1},{5,3},{7,5},{10,8},{12,10},{14,12},{11,9},... | collective-permute-start | bytes 196616 | tf_op jit(solution)/shard_map/ppermute | solution.py:41
  19.0 57.1 %collective-permute-start.2 = (bf16[4,4,32,2560]{3,2,1,0:T(8,128)(2,1)S(1)}, bf16[4,4,32,2560]{3,2,1,0:T(8,128)(2,1)}, u32[]{:S(2)}, u32[]{:S(2)}) collective-permute-start(bf16[4,4,32,2560]{3,2,1,0:T(8,128)(2,1)S(1)} %broadcast_select_fusion.3), channel_id=1, source_target_pairs={{0,1},{1,0},{2,3},{3,2},{4,5},{5,4},{6,7},{7,6},{8,9},{9,8},{10,11... | collective-permute-start | bytes 7864328 | tf_op jit(solution)/shard_map/ppermute | solution.py:16
  22.4 53.7 %slice-start.2 = ((s8[5242880]{0:T(1024)(128)(4,1)}), s8[4194304]{0:T(1024)(128)(4,1)S(1)}, s32[]{:S(2)}) async-start(s8[5242880]{0:T(1024)(128)(4,1)} %bitcast.115), calls=%async_computation.3 | async-start | bytes 8388608
  23.0 53.1 %slice-start.3 = ((s8[5242880]{0:T(1024)(128)(4,1)}), s8[1048576]{0:T(1024)(128)(4,1)S(1)}, s32[]{:S(2)}) async-start(s8[5242880]{0:T(1024)(128)(4,1)} %bitcast.115), calls=%async_computation.4 | async-start | bytes 2097152
  23.8 54.3 %copy-start.9 = (bf16[8,4,32,3456]{3,2,1,0:T(8,128)(2,1)}, bf16[8,4,32,3456]{3,2,1,0:T(8,128)(2,1)S(1)}, u32[]{:S(2)}) copy-start(bf16[8,4,32,3456]{3,2,1,0:T(8,128)(2,1)S(1)} %slice_dynamic-update-slice_fusion) | copy-start | bytes 21233668
  107.8 41.7 %collective-permute-start.21 = (bf16[4,2,216,768]{3,2,1,0:T(8,128)(2,1)}, bf16[4,2,216,768]{3,2,1,0:T(8,128)(2,1)}, u32[]{:S(2)}, u32[]{:S(2)}) collective-permute-start(bf16[4,2,216,768]{3,2,1,0:T(8,128)(2,1)} %fusion.12), channel_id=1, source_target_pairs={{0,2},{2,0},{4,6},{6,4},{1,3},{3,1},{5,7},{7,5},{8,10},{10,8},{12,... | collective-permute-start | bytes 7962632 | tf_op jit(solution)/shard_map/ppermute | solution.py:16
  116.7 40.9 %collective-permute-start.4 = (bf16[4,2,216,896]{3,2,0,1:T(8,128)(2,1)}, bf16[4,2,216,896]{3,2,0,1:T(8,128)(2,1)}, u32[]{:S(2)}, u32[]{:S(2)}) collective-permute-start(bf16[4,2,216,896]{3,2,0,1:T(8,128)(2,1)} %bitcast.108), channel_id=1, source_target_pairs={{0,2},{2,0},{4,6},{6,4},{1,3},{3,1},{5,7},{7,5},{8,10},{10,8},{12,... | collective-permute-start | bytes 9289736 | tf_op jit(solution)/shard_map/ppermute | solution.py:16
  118.7 4.7 %collective-permute-start.5 = (f32[2560]{0:T(1024)S(1)}, f32[2560]{0:T(1024)S(1)}, u32[]{:S(2)}, u32[]{:S(2)}) collective-permute-start(f32[2560]{0:T(1024)S(1)} %convert_reduce_fusion), channel_id=1, source_target_pairs={{0,8},{8,0},{16,24},{24,16},{1,9},{9,1},{17,25},{25,17},{2,10},{10... | collective-permute-start | bytes 30728 | tf_op jit(solution)/shard_map/ppermute | solution.py:16
  123.4 14.6 %collective-permute-start.6 = (f32[2560]{0:T(1024)S(1)}, f32[2560]{0:T(1024)S(1)}, u32[]{:S(2)}, u32[]{:S(2)}) collective-permute-start(f32[2560]{0:T(1024)S(1)} %add.352), channel_id=1, source_target_pairs={{0,16},{8,24},{16,0},{24,8},{1,17},{9,25},{17,1},{25,9},{2,18},{10... | collective-permute-start | bytes 30728 | tf_op jit(solution)/shard_map/ppermute | solution.py:16
  137.4 102.0 %collective-permute-start.16 = (bf16[4,2,216,896]{3,2,0,1:T(8,128)(2,1)}, bf16[4,2,216,896]{3,2,0,1:T(8,128)(2,1)}, u32[]{:S(2)}, u32[]{:S(2)}) collective-permute-start(bf16[4,2,216,896]{3,2,0,1:T(8,128)(2,1)} %bitcast.109), channel_id=1, source_target_pairs={{0,2},{2,0},{4,6},{6,4},{1,3},{3,1},{5,7},{7,5},{8,10},{10,8},{12,... | collective-permute-start | bytes 9289736 | tf_op jit(solution)/shard_map/ppermute | solution.py:16
  138.0 7.2 %collective-permute-start.7 = (f32[2560]{0:T(1024)S(1)}, f32[2560]{0:T(1024)S(1)}, u32[]{:S(2)}, u32[]{:S(2)}) collective-permute-start(f32[2560]{0:T(1024)S(1)} %add.353), channel_id=1, source_target_pairs={{0,2},{2,0},{4,6},{6,4},{1,3},{3,1},{5,7},{7,5},{8,10},{10,8},{12,... | collective-permute-start | bytes 30728 | tf_op jit(solution)/shard_map/ppermute | solution.py:16
  145.2 3.1 collective-permute-start.8
  154.9 74.7 %collective-permute-start.22 = (bf16[2,216,768]{2,1,0:T(8,128)(2,1)}, bf16[2,216,768]{2,1,0:T(8,128)(2,1)}, u32[]{:S(2)}, u32[]{:S(2)}) collective-permute-start(bf16[2,216,768]{2,1,0:T(8,128)(2,1)} %get-tuple-element.39), channel_id=1, source_target_pairs={{0,8},{8,0},{16,24},{24,16},{1,9},{9,1},{17,25},{25,17},{2,10},{10... | collective-permute-start | bytes 1990664 | tf_op jit(solution)/shard_map/ppermute | solution.py:16
  155.5 74.1 %collective-permute-start.24 = (bf16[2,216,768]{2,1,0:T(8,128)(2,1)}, bf16[2,216,768]{2,1,0:T(8,128)(2,1)}, u32[]{:S(2)}, u32[]{:S(2)}) collective-permute-start(bf16[2,216,768]{2,1,0:T(8,128)(2,1)} %get-tuple-element.40), channel_id=1, source_target_pairs={{0,24},{8,16},{16,8},{24,0},{1,25},{9,17},{17,9},{25,1},{2,26},{10... | collective-permute-start | bytes 1990664 | tf_op jit(solution)/shard_map/ppermute | solution.py:16
  156.1 73.5 %collective-permute-start.23 = (bf16[2,216,768]{2,1,0:T(8,128)(2,1)}, bf16[2,216,768]{2,1,0:T(8,128)(2,1)}, u32[]{:S(2)}, u32[]{:S(2)}) collective-permute-start(bf16[2,216,768]{2,1,0:T(8,128)(2,1)} %get-tuple-element.41), channel_id=1, source_target_pairs={{0,16},{8,24},{16,0},{24,8},{1,17},{9,25},{17,1},{25,9},{2,18},{10... | collective-permute-start | bytes 1990664 | tf_op jit(solution)/shard_map/ppermute | solution.py:16
  162.9 33.2 %collective-permute-start.9 = (bf16[4,216,896]{2,1,0:T(8,128)(2,1)S(1)}, bf16[4,216,896]{2,1,0:T(8,128)(2,1)S(1)}, u32[]{:S(2)}, u32[]{:S(2)}) collective-permute-start(bf16[4,216,896]{2,1,0:T(8,128)(2,1)S(1)} %fusion.14), channel_id=1, source_target_pairs={{0,4},{2,6},{4,0},{6,2},{1,5},{3,7},{5,1},{7,3},{8,12},{10,14},{12... | collective-permute-start | bytes 4644872 | tf_op jit(solution)/shard_map/ppermute | solution.py:16
  196.1 138.7 %collective-permute-start.3 = (bf16[4,4,32,2560]{3,2,1,0:T(8,128)(2,1)}, bf16[4,4,32,2560]{3,2,1,0:T(8,128)(2,1)}, u32[]{:S(2)}, u32[]{:S(2)}) collective-permute-start(bf16[4,4,32,2560]{3,2,1,0:T(8,128)(2,1)} %broadcast_select_fusion.1), channel_id=1, source_target_pairs={{0,1},{1,0},{2,3},{3,2},{4,5},{5,4},{6,7},{7,6},{8,9},{9,8},{10,11... | collective-permute-start | bytes 7864328 | tf_op jit(solution)/shard_map/ppermute | solution.py:16
  232.1 48.9 %collective-permute-start.25 = (bf16[216,768]{1,0:T(8,128)(2,1)S(1)}, bf16[216,768]{1,0:T(8,128)(2,1)}, u32[]{:S(2)}, u32[]{:S(2)}) collective-permute-start(bf16[216,768]{1,0:T(8,128)(2,1)S(1)} %fusion.50), channel_id=1, source_target_pairs={{0,4},{2,6},{4,0},{6,2},{1,5},{3,7},{5,1},{7,3},{8,12},{10,14},{12... | collective-permute-start | bytes 995336 | tf_op jit(solution)/shard_map/ppermute | solution.py:16
  242.3 41.1 %collective-permute-start.17 = (bf16[4,216,896]{2,1,0:T(8,128)(2,1)S(1)}, bf16[4,216,896]{2,1,0:T(8,128)(2,1)S(1)}, u32[]{:S(2)}, u32[]{:S(2)}) collective-permute-start(bf16[4,216,896]{2,1,0:T(8,128)(2,1)S(1)} %fusion.15), channel_id=1, source_target_pairs={{0,4},{2,6},{4,0},{6,2},{1,5},{3,7},{5,1},{7,3},{8,12},{10,14},{12... | collective-permute-start | bytes 4644872 | tf_op jit(solution)/shard_map/ppermute | solution.py:16
  248.5 26.6 %collective-permute-start.10 = (f32[8,1,32,128]{3,2,1,0:T(8,128)S(1)}, f32[8,1,32,128]{3,2,1,0:T(8,128)S(1)}, u32[]{:S(2)}, u32[]{:S(2)}) collective-permute-start(f32[8,1,32,128]{3,2,1,0:T(8,128)S(1)} %get-tuple-element.48), channel_id=1, source_target_pairs={{0,2},{2,4},{4,6},{1,3},{3,5},{5,7},{8,10},{10,12},{12,14},{9,11},... | collective-permute-start | bytes 393224 | tf_op jit(solution)/shard_map/ppermute | solution.py:41
  255.0 24.4 %collective-permute-start.11 = (f32[8,1,32,128]{3,2,1,0:T(8,128)S(1)}, f32[8,1,32,128]{3,2,1,0:T(8,128)S(1)}, u32[]{:S(2)}, u32[]{:S(2)}) collective-permute-start(f32[8,1,32,128]{3,2,1,0:T(8,128)S(1)} %get-tuple-element.49), channel_id=1, source_target_pairs={{2,0},{4,2},{6,4},{3,1},{5,3},{7,5},{10,8},{12,10},{14,12},{11,9},... | collective-permute-start | bytes 393224 | tf_op jit(solution)/shard_map/ppermute | solution.py:41
  275.1 10.1 %collective-permute-start.13 = (bf16[216,896]{1,0:T(8,128)(2,1)S(1)}, bf16[216,896]{1,0:T(8,128)(2,1)S(1)}, u32[]{:S(2)}, u32[]{:S(2)}) collective-permute-start(bf16[216,896]{1,0:T(8,128)(2,1)S(1)} %get-tuple-element.42), channel_id=1, source_target_pairs={{0,8},{8,0},{16,24},{24,16},{1,9},{9,1},{17,25},{25,17},{2,10},{10... | collective-permute-start | bytes 1161224 | tf_op jit(solution)/shard_map/ppermute | solution.py:16
  279.4 11.9 %collective-permute-start.15 = (bf16[216,896]{1,0:T(8,128)(2,1)S(1)}, bf16[216,896]{1,0:T(8,128)(2,1)S(1)}, u32[]{:S(2)}, u32[]{:S(2)}) collective-permute-start(bf16[216,896]{1,0:T(8,128)(2,1)S(1)} %get-tuple-element.43), channel_id=1, source_target_pairs={{0,24},{8,16},{16,8},{24,0},{1,25},{9,17},{17,9},{25,1},{2,26},{10... | collective-permute-start | bytes 1161224 | tf_op jit(solution)/shard_map/ppermute | solution.py:16
  281.1 38.8 %collective-permute-start.14 = (bf16[216,896]{1,0:T(8,128)(2,1)S(1)}, bf16[216,896]{1,0:T(8,128)(2,1)S(1)}, u32[]{:S(2)}, u32[]{:S(2)}) collective-permute-start(bf16[216,896]{1,0:T(8,128)(2,1)S(1)} %get-tuple-element.44), channel_id=1, source_target_pairs={{0,16},{8,24},{16,0},{24,8},{1,17},{9,25},{17,1},{25,9},{2,18},{10... | collective-permute-start | bytes 1161224 | tf_op jit(solution)/shard_map/ppermute | solution.py:16
  283.5 36.6 %collective-permute-start.12 = (f32[8,4,32,128]{3,2,1,0:T(8,128)S(1)}, f32[8,4,32,128]{3,2,1,0:T(8,128)S(1)}, u32[]{:S(2)}, u32[]{:S(2)}) collective-permute-start(f32[8,4,32,128]{3,2,1,0:T(8,128)S(1)} %slice_add_fusion), channel_id=1, source_target_pairs={{0,1},{1,0},{2,3},{3,2},{4,5},{5,4},{6,7},{7,6},{8,9},{9,8},{10,11... | collective-permute-start | bytes 1572872 | tf_op jit(solution)/shard_map/ppermute | solution.py:16
  284.7 50.1 %slice-start.4 = ((s8[5242880]{0:T(1024)(128)(4,1)}), s8[4194304]{0:T(1024)(128)(4,1)S(1)}, s32[]{:S(2)}) async-start(s8[5242880]{0:T(1024)(128)(4,1)} %bitcast.118), calls=%async_computation.5 | async-start | bytes 8388608
  285.0 35.1 %copy-start.8 = (bf16[1,8,4,32,128]{4,3,2,1,0:T(8,128)(2,1)S(1)}, bf16[1,8,4,32,128]{4,3,2,1,0:T(8,128)(2,1)}, u32[]{:S(2)}) copy-start(bf16[1,8,4,32,128]{4,3,2,1,0:T(8,128)(2,1)} %param.5) | copy-start | bytes 786436
  285.2 35.9 %collective-permute-start.18 = (bf16[216,896]{1,0:T(8,128)(2,1)S(1)}, bf16[216,896]{1,0:T(8,128)(2,1)S(1)}, u32[]{:S(2)}, u32[]{:S(2)}) collective-permute-start(bf16[216,896]{1,0:T(8,128)(2,1)S(1)} %get-tuple-element.45), channel_id=1, source_target_pairs={{0,8},{8,0},{16,24},{24,16},{1,9},{9,1},{17,25},{25,17},{2,10},{10... | collective-permute-start | bytes 1161224 | tf_op jit(solution)/shard_map/ppermute | solution.py:16
  291.2 29.8 %collective-permute-start.20 = (bf16[216,896]{1,0:T(8,128)(2,1)S(1)}, bf16[216,896]{1,0:T(8,128)(2,1)S(1)}, u32[]{:S(2)}, u32[]{:S(2)}) collective-permute-start(bf16[216,896]{1,0:T(8,128)(2,1)S(1)} %get-tuple-element.46), channel_id=1, source_target_pairs={{0,24},{8,16},{16,8},{24,0},{1,25},{9,17},{17,9},{25,1},{2,26},{10... | collective-permute-start | bytes 1161224 | tf_op jit(solution)/shard_map/ppermute | solution.py:16
  319.8 13.1 %collective-permute-start.19 = (bf16[216,896]{1,0:T(8,128)(2,1)S(1)}, bf16[216,896]{1,0:T(8,128)(2,1)S(1)}, u32[]{:S(2)}, u32[]{:S(2)}) collective-permute-start(bf16[216,896]{1,0:T(8,128)(2,1)S(1)} %get-tuple-element.47), channel_id=1, source_target_pairs={{0,16},{8,24},{16,0},{24,8},{1,17},{9,25},{17,1},{25,9},{2,18},{10... | collective-permute-start | bytes 1161224 | tf_op jit(solution)/shard_map/ppermute | solution.py:16
  (17 other events, 115.7 us)
Sparse Core Ops, SparseCore 0:
  9.6 95.8 all-gather.1
